TPU v7x, 256 devices: a whole 4x4x8 slice. The times are simulated.
256 devices in a mesh: ep: 8 (over y, core), tm: 32 (over z, x).
Axes of the slice: x: 4, y: 4, z: 8, core: 2. Of those that a mesh axis runs over, the one named last changes fastest.
Arguments:
- observed: float32 [2048, 4096, 32], P('ep', 'tm'), may hold values from -27 to 27
- missing: int32 [2048, 4096, 32], P('ep', 'tm'), may hold values 0 or 1
- episode_init: float32 [2048, 256], P(('ep', 'tm')), may hold values from -2 to 2
- time_init: float32 [4096, 256], P(('tm', 'ep')), may hold values from -2 to 2
- channel: float32 [32, 256], replicated, may hold values from -0.5 to 1.5
Outputs:
- imputed: float32 [2048, 4096, 32], P('ep', 'tm')
All inputs are finite; a program needn't handle non-finite values. No bound on the sum of `missing` on one device may be relied on, other than what follows from the above.
Results may differ from a plain program's by a relative error of at most 0.0003.
Values sent between devices are 32-bit elements; how exact they have to be, the bound alone decides.
A program may use at most 128 MiB of HBM per device.

v0:
```python
import jax
import jax.numpy as jnp
from jax import lax
from jax.sharding import PartitionSpec as P

SWEEPS = 2


ridge_weight = 1.0
HIGH = lax.Precision.HIGHEST


def khatri(left, channel):
    return (left[:, None, :] * channel[None, :, :]).reshape(-1, left.shape[1])


def gram_rows(rows):
    return lax.dot_general(
        rows, rows, (((0,), (0,)), ((), ())), precision=HIGH, preferred_element_type=jnp.float32
    )


def solve_rows(lower, moments):
    return jax.scipy.linalg.cho_solve((lower, True), moments.T).T


def system_factor(gram_other, gram_c):
    system = gram_other * gram_c + ridge_weight * jnp.eye(gram_c.shape[0], dtype=jnp.float32)
    return jnp.linalg.cholesky(system)


def shard_gram(own_rows):
    return lax.psum(gram_rows(own_rows), ("ep", "tm"))


def on_device(observed, missing, episode_init, time_init, channel):
    i_blk, j_blk, width = observed.shape
    rank = channel.shape[1]
    flat_obs = observed.reshape(i_blk, j_blk * width)
    flat_miss = missing.reshape(i_blk, j_blk * width)
    gram_c = gram_rows(channel)
    b_count = time_init.shape[0]

    def gather_episode(rows):
        return lax.all_gather(rows, "tm", axis=0, tiled=True)

    def gather_time(rows):
        return lax.all_gather(rows, "ep", axis=0, tiled=True)

    def complete(a_block, basis):
        model = lax.dot_general(
            a_block,
            basis,
            (((1,), (1,)), ((), ())),
            precision=HIGH,
            preferred_element_type=jnp.float32,
        )
        return jnp.where(flat_miss == 1, model, flat_obs)

    a_own = episode_init
    b_own = time_init
    a_block = gather_episode(a_own)
    b_block = gather_time(b_own)
    for sweep in range(SWEEPS):
        basis = khatri(b_block, channel)
        filled = complete(a_block, basis)
        lower_e = system_factor(shard_gram(b_own), gram_c)
        moments_e = lax.psum_scatter(
            jnp.dot(filled, basis, precision=HIGH, preferred_element_type=jnp.float32),
            "tm",
            scatter_dimension=0,
            tiled=True,
        )
        a_own = solve_rows(lower_e, moments_e)
        a_block = gather_episode(a_own)
        filled_cube = filled.reshape(i_blk, j_blk, width)
        lower_t = system_factor(shard_gram(a_own), gram_c)
        columns = filled_cube.reshape(i_blk, lax.axis_size("ep") * b_count * width)
        part = lax.dot_general(
            columns,
            a_block,
            (((0,), (0,)), ((), ())),
            precision=HIGH,
            preferred_element_type=jnp.float32,
        )
        moments_t = lax.psum_scatter(
            jnp.sum(
                part.reshape(lax.axis_size("ep") * b_count, width, rank) * channel[None, :, :],
                axis=1,
            ),
            "ep",
            scatter_dimension=0,
            tiled=True,
        )
        b_own = solve_rows(lower_t, moments_t)
        b_block = gather_time(b_own)
    basis = khatri(b_block, channel)
    filled = complete(a_block, basis)
    return filled.reshape(i_blk, j_blk, width)


def solution(mesh):
    in_specs = (
        P("ep", "tm", None),
        P("ep", "tm", None),
        P(("ep", "tm"), None),
        P(("tm", "ep"), None),
        P(),
    )
    out_specs = P("ep", "tm", None)
    return jax.shard_map(
        on_device, mesh=mesh, in_specs=in_specs, out_specs=out_specs, check_vma=False
    )
```

profile of v0, /device:TPU:1, one launch (start us, length us, event | category | flops | bytes accessed | tf_op | source)
XLA Modules:
  0.0 1333.3 jit_solution(5304896017590537827)
XLA Ops:
  7.4 1.9 fusion.66
  9.4 16.0 %all_gather.18 = f32[128,256]{1,0:T(8,128)S(1)} all-gather(f32[16,256]{1,0:T(8,128)} %param.13), channel_id=1, replica_groups=mesh['ep'=8,'tm'=32] {'ep'}, dimensions={0}, use_global_device_ids=true | all-gather | bytes 147456 | tf_op jit(solution)/shard_map/all_gather | solution.py:48
  25.4 5.5 copy.10
  30.9 2.8 broadcast_compare_fusion
  33.8 5.8 copy.6
  39.5 39.6 %all_gather.19 = f32[256,256]{1,0:T(8,128)S(1)} all-gather(f32[8,256]{1,0:T(8,128)S(1)} %copy-done.6), channel_id=1, replica_groups=mesh['ep'=8,'tm'=32] {'tm'}, dimensions={0}, use_global_device_ids=true | all-gather | bytes 270336 | tf_op jit(solution)/shard_map/all_gather | solution.py:45
  79.7 3.5 fusion
  83.2 1.9 copy-done.3
  85.1 7.4 fusion.67
  93.1 175.3 %all-reduce.6.cloned.1.call-done = f32[256,256]{0,1:T(8,128)} async-done(((f32[256,256]{0,1:T(8,128)}), f32[256,256]{0,1:T(8,128)}) %all-reduce.6.cloned.1.call-update) | async-done | bytes 262160 | tf_op jit(solution)/shard_map/psum | solution.py:33
  269.9 11.7 cholesky.214
  281.7 9.8 custom-call.23
  292.0 11.7 cholesky.231
  305.9 4.1 while.8
  310.0 19.7 %custom-call.24 = f32[2,128,128]{1,2,0:T(8,128)S(1)} custom-call(f32[2,128,128]{2,1,0:T(8,128)S(1)} %get-tuple-element.36), custom_call_target="InvertDiagBlocksLowerTriangular" | custom-call | tf_op jit(solution)/shard_map/jit(_cho_solve)/triangular_solve | solution.py:24
  333.6 39.4 %all_gather.20 = f32[256,256]{1,0:T(8,128)S(1)} all-gather(f32[8,256]{1,0:T(8,128)S(1)} %fusion.55), channel_id=1, replica_groups=mesh['ep'=8,'tm'=32] {'tm'}, dimensions={0}, use_global_device_ids=true | all-gather | bytes 270336 | tf_op jit(solution)/shard_map/all_gather | solution.py:45
  373.0 6.3 multiply_reduce_fusion.1
  379.6 203.0 %all-reduce.8.cloned.1.call-done = f32[256,256]{0,1:T(8,128)} async-done(((f32[256,256]{0,1:T(8,128)}), f32[256,256]{0,1:T(8,128)}) %all-reduce.8.cloned.1.call-update) | async-done | bytes 262160 | tf_op jit(solution)/shard_map/psum | solution.py:33
  583.8 11.7 cholesky.248
  595.6 9.8 custom-call.25
  605.8 11.7 cholesky.265
  620.5 4.8 while.9
  621.6 1.5 bitcast_dynamic-update-slice_fusion.9
  623.7 1.5 bitcast_dynamic-update-slice_fusion.9
  625.2 19.7 %custom-call.26 = f32[2,128,128]{1,2,0:T(8,128)S(1)} custom-call(f32[2,128,128]{2,1,0:T(8,128)S(1)} %get-tuple-element.37), custom_call_target="InvertDiagBlocksLowerTriangular" | custom-call | tf_op jit(solution)/shard_map/jit(_cho_solve)/triangular_solve | solution.py:24
  648.8 15.0 %all_gather.21 = f32[128,256]{1,0:T(8,128)S(1)} all-gather(f32[16,256]{1,0:T(8,128)S(1)} %fusion.49), channel_id=1, replica_groups=mesh['ep'=8,'tm'=32] {'ep'}, dimensions={0}, use_global_device_ids=true | all-gather | bytes 147456 | tf_op jit(solution)/shard_map/all_gather | solution.py:48
  664.4 2.0 copy-done.4
  666.4 5.0 convolution_select_fusion.1
  671.5 10.9 fusion.68
  682.7 237.1 %all-reduce.10.cloned.1.call-done = f32[256,256]{0,1:T(8,128)} async-done(((f32[256,256]{0,1:T(8,128)}), f32[256,256]{0,1:T(8,128)}) %all-reduce.10.cloned.1.call-update) | async-done | bytes 262160 | tf_op jit(solution)/shard_map/psum | solution.py:33
  921.0 11.7 cholesky.282
  932.7 9.8 custom-call.27
  943.0 11.7 cholesky.299
  957.3 3.8 while.10
  961.1 19.7 %custom-call.28 = f32[2,128,128]{1,2,0:T(8,128)S(1)} custom-call(f32[2,128,128]{2,1,0:T(8,128)S(1)} %get-tuple-element.38), custom_call_target="InvertDiagBlocksLowerTriangular" | custom-call | tf_op jit(solution)/shard_map/jit(_cho_solve)/triangular_solve | solution.py:24
  984.8 39.3 %all_gather.22 = f32[256,256]{1,0:T(8,128)S(1)} all-gather(f32[8,256]{1,0:T(8,128)S(1)} %fusion.54), channel_id=1, replica_groups=mesh['ep'=8,'tm'=32] {'tm'}, dimensions={0}, use_global_device_ids=true | all-gather | bytes 270336 | tf_op jit(solution)/shard_map/all_gather | solution.py:45
  1024.1 6.3 multiply_reduce_fusion
  1030.4 203.3 %all-reduce.12.cloned.1.call-done = f32[256,256]{0,1:T(8,128)} async-done(((f32[256,256]{0,1:T(8,128)}), f32[256,256]{0,1:T(8,128)}) %all-reduce.12.cloned.1.call-update) | async-done | bytes 262160 | tf_op jit(solution)/shard_map/psum | solution.py:33
  1234.9 11.7 cholesky.316
  1246.6 9.8 custom-call.29
  1256.9 11.9 cholesky.333
  1271.8 4.3 while.11
  1272.4 1.5 bitcast_dynamic-update-slice_fusion.11
  1274.6 1.5 bitcast_dynamic-update-slice_fusion.11
  1276.1 19.7 %custom-call.30 = f32[2,128,128]{1,2,0:T(8,128)S(1)} custom-call(f32[2,128,128]{2,1,0:T(8,128)S(1)} %get-tuple-element.39), custom_call_target="InvertDiagBlocksLowerTriangular" | custom-call | tf_op jit(solution)/shard_map/jit(_cho_solve)/triangular_solve | solution.py:24
  1298.9 14.9 %all_gather.23 = f32[128,256]{1,0:T(8,128)S(1)} all-gather(f32[16,256]{1,0:T(8,128)S(1)} %maximum_bitcast_fusion), channel_id=1, replica_groups=mesh['ep'=8,'tm'=32] {'ep'}, dimensions={0}, use_global_device_ids=true | all-gather | bytes 147456 | tf_op jit(solution)/shard_map/all_gather | solution.py:48
  1314.4 5.1 convolution_select_fusion
  1319.5 5.9 copy.22
  (139 shorter events, 40.4 us)
Async XLA Ops:
  7.4 261.0 %all-reduce.6.cloned.1.call-start = ((), (), s32[]{:S(2)}) async-start(), calls=%async_computation.4 | async-start | bytes 524288 | tf_op jit(solution)/shard_map/psum | solution.py:33
  9.3 320.4 %reduce-scatter.5.cloned.1.call-start = ((), (), s32[]{:S(2)}) async-start(), calls=%async_computation.5 | async-start | bytes 270336 | tf_op jit(solution)/shard_map/reduce_scatter | solution.py:68
  30.9 8.6 copy-start.6
  30.9 48.2 %copy-start.5 = (f32[32,256]{1,0:T(8,128)S(1)}, f32[32,256]{1,0:T(8,128)}, u32[]{:S(2)}) copy-start(f32[32,256]{1,0:T(8,128)} %param.14) | copy-start | bytes 98308
  33.7 46.0 %copy-start = (f32[256,128,32]{0,2,1:T(8,128)S(1)}, f32[256,128,32]{0,2,1:T(8,128)}, u32[]{:S(2)}) copy-start(f32[256,128,32]{0,2,1:T(8,128)} %copy.10) | copy-start | bytes 12582916
  83.2 1.9 copy-start.3
  92.6 490.0 %all-reduce.8.cloned.1.call-start = ((), (), s32[]{:S(2)}) async-start(), calls=%async_computation.6 | async-start | bytes 524288 | tf_op jit(solution)/shard_map/psum | solution.py:33
  333.6 311.4 %reduce-scatter.7.cloned.1.call-start = ((), (), s32[]{:S(2)}) async-start(), calls=%async_computation.7 | async-start | bytes 147456 | tf_op jit(solution)/shard_map/reduce_scatter | solution.py:86
  379.3 540.4 %all-reduce.10.cloned.1.call-start = ((), (), s32[]{:S(2)}) async-start(), calls=%async_computation.8 | async-start | bytes 524288 | tf_op jit(solution)/shard_map/psum | solution.py:33
  648.8 17.6 %copy-start.1 = (f32[256,128,32]{0,2,1:T(8,128)S(1)}, f32[256,128,32]{0,2,1:T(8,128)}, u32[]{:S(2)}) copy-start(f32[256,128,32]{0,2,1:T(8,128)} %copy.10) | copy-start | bytes 12582916
  664.4 2.0 copy-start.4
  671.5 309.4 %reduce-scatter.9.cloned.1.call-start = ((), (), s32[]{:S(2)}) async-start(), calls=%async_computation.9 | async-start | bytes 270336 | tf_op jit(solution)/shard_map/reduce_scatter | solution.py:68
  682.5 551.2 %all-reduce.12.cloned.1.call-start = ((), (), s32[]{:S(2)}) async-start(), calls=%async_computation.10 | async-start | bytes 524288 | tf_op jit(solution)/shard_map/psum | solution.py:33
  984.7 311.1 %reduce-scatter.11.cloned.1.call-start = ((), (), s32[]{:S(2)}) async-start(), calls=%async_computation.11 | async-start | bytes 147456 | tf_op jit(solution)/shard_map/reduce_scatter | solution.py:86
  1295.8 18.7 %copy-start.2 = (f32[256,128,32]{0,2,1:T(8,128)S(1)}, f32[256,128,32]{0,2,1:T(8,128)}, u32[]{:S(2)}) copy-start(f32[256,128,32]{0,2,1:T(8,128)} %copy.10) | copy-start | bytes 12582916
Sparse Core Ops, SparseCore 0:
  13.6 254.6 all-reduce.5
  333.7 248.8 all-reduce.7
  585.2 30.8 reduce-scatter.6
  671.6 248.1 all-reduce.9
  984.8 248.8 all-reduce.11
  1236.2 30.8 reduce-scatter.10
Sparse Core Ops, SparseCore 1:
  92.7 216.5 reduce-scatter.4
  682.6 206.1 reduce-scatter.8
where the time goes:
time: 1340 us; the launch traced here: 1330 us
  waiting for transfers between devices  819 us (61%)
  other arithmetic  225 us (17%)
  blocking collectives  164 us (12%)
  matrix products  64.3 us (5%)
  local copies, waits for them, and re-layouts  38 us (3%)
  between operations  21.1 us (2%)
    psum x4, waiting for transfers between devices, shard_gram(): return lax.psum(gram_rows(own_rows), ('ep', 'tm'))  819 us
    another operation x27, other arithmetic, system_factor(): return jnp.linalg.cholesky(system)  138 us
    all_gather x3, blocking collectives, gather_episode(): return lax.all_gather(rows, 'tm', axis=0, tiled=True)  118 us
    another operation x9, other arithmetic, solve_rows(): return jax.scipy.linalg.cho_solve((lower, True), moments.T).T  78.8 us
    all_gather x3, blocking collectives, gather_time(): return lax.all_gather(rows, 'ep', axis=0, tiled=True)  46 us
  transfers between devices with their start and end apart: 8, of which 4 were waited for; matrix products, arithmetic and copies ran while one was open for 22% of the time, Pallas kernels for 0%

commit v1 on v0

v1 whole, which is shorter than its diff:
```python
import functools

import jax
import jax.numpy as jnp
from jax import lax
from jax.experimental import pallas as pl
from jax.experimental.pallas import tpu as pltpu
from jax.sharding import PartitionSpec as P

SWEEPS = 2
RIDGE = 1.0
HIGH = lax.Precision.HIGHEST
F32 = jnp.float32
BF16 = jnp.bfloat16
MESH = pl.DeviceIdType.MESH

RANK = 256
WIDTH = 32
N_EP = 8
N_TM = 32
N_X = 4
I_BLK = 256
J_BLK = 128
ROWS = I_BLK * WIDTH
STEP_I = 8
CHUNK = STEP_I * WIDTH
N_CHUNK = ROWS // CHUNK
A_OWN = 8
B_OWN = 16
PIECE = 8
VMEM_LIMIT = 56 * 1024 * 1024


def dot(left, right):
    return lax.dot_general(
        left, right, (((1,), (0,)), ((), ())), preferred_element_type=F32
    )


def dot_high(left, right):
    return lax.dot_general(
        left, right, (((1,), (0,)), ((), ())), precision=HIGH, preferred_element_type=F32
    )


def split2(x):
    high = x.astype(BF16)
    return high, (x - high.astype(F32)).astype(BF16)


def split3(x):
    high = x.astype(BF16)
    rest = x - high.astype(F32)
    mid = rest.astype(BF16)
    return high, mid, (rest - mid.astype(F32)).astype(BF16)


def dot_packed(left, right):
    a0, a1, a2 = split3(left)
    b0, b1, b2 = split3(right)
    lhs = jnp.concatenate([a0, a0, a1, a0, a2, a1], axis=1)
    rhs = jnp.concatenate([b0, b1, b0, b2, b0, b1], axis=0)
    return dot(lhs, rhs)


def invert8(cols):
    row = lax.broadcasted_iota(jnp.int32, (8, 128), 0)
    for s in range(8):
        here = row == s
        at_s = [jnp.broadcast_to(cols[q][s : s + 1, :], (8, 128)) for q in range(8)]
        inv = 1.0 / at_s[s]
        pivot = cols[s]
        fresh = []
        for q in range(8):
            if q == s:
                fresh.append(jnp.where(here, inv, -pivot * inv))
            else:
                scaled = at_s[q] * inv
                fresh.append(jnp.where(here, scaled, cols[q] - pivot * scaled))
        cols = fresh
    return cols


def spread_row(x, m):
    return jnp.broadcast_to(x[m : m + 1, :], (8, 128))


def eliminate_panel(ref, r0, depth, n):
    tiles = n // 128
    groups = depth // 8
    lane = lax.broadcasted_iota(jnp.int32, (8, 128), 1)
    row = lax.broadcasted_iota(jnp.int32, (8, 128), 0)
    x = [
        [ref[r0 + 8 * v : r0 + 8 * v + 8, 128 * t : 128 * t + 128] for t in range(tiles)]
        for v in range(groups)
    ]
    for g in range(groups):
        t_piv, l0 = divmod(r0 + 8 * g, 128)

        def column(block, q):
            return jnp.broadcast_to(block[:, l0 + q : l0 + q + 1], (8, 128))

        inv = invert8([column(x[g][t_piv], q) for q in range(8)])
        inside = (lane >= l0) & (lane < l0 + 8)
        unit = jnp.where(lane - l0 == row, 1.0, 0.0)
        fresh = []
        for t in range(tiles):
            old = x[g][t]
            if t == t_piv:
                old = jnp.where(inside, unit, old)
            y = [inv[m] * spread_row(old, m) for m in range(8)]
            fresh.append(((y[0] + y[1]) + (y[2] + y[3])) + ((y[4] + y[5]) + (y[6] + y[7])))
        for v in range(groups):
            if v == g:
                continue
            cols = [column(x[v][t_piv], m) for m in range(8)]
            for t in range(tiles):
                old = x[v][t]
                if t == t_piv:
                    old = jnp.where(inside, 0.0, old)
                y = [cols[m] * spread_row(fresh[t], m) for m in range(8)]
                x[v][t] = old - (
                    ((y[0] + y[1]) + (y[2] + y[3])) + ((y[4] + y[5]) + (y[6] + y[7]))
                )
        x[g] = fresh
    for v in range(groups):
        for t in range(tiles):
            ref[r0 + 8 * v : r0 + 8 * v + 8, 128 * t : 128 * t + 128] = x[v][t]


def invert_in_place(ref, n, depth):
    for k in range(n // depth):
        r0 = k * depth
        eliminate_panel(ref, r0, depth, n)
        panel = ref[r0 : r0 + depth, :]
        lane = lax.broadcasted_iota(jnp.int32, (1, n), 1)
        inside = (lane >= r0) & (lane < r0 + depth)
        for lo, hi in ((0, r0), (r0 + depth, n)):
            if hi > lo:
                cols = ref[lo:hi, r0 : r0 + depth]
                ref[lo:hi, :] = jnp.where(inside, 0.0, ref[lo:hi, :]) - dot_packed(cols, panel)


def solve_kernel(g_ref, gc_ref, m_ref, out_ref, s_ref):
    n = RANK
    eye = lax.broadcasted_iota(jnp.int32, (n, n), 0) == lax.broadcasted_iota(jnp.int32, (n, n), 1)
    s_ref[...] = g_ref[...] * gc_ref[...] + jnp.where(eye, RIDGE, 0.0)
    invert_in_place(s_ref, n, 32)
    out_ref[...] = dot_high(m_ref[...], s_ref[...])


def solve_rows(gram, gram_c, moments):
    return pl.pallas_call(
        solve_kernel,
        out_shape=jax.ShapeDtypeStruct(moments.shape, F32),
        in_specs=[pl.BlockSpec(memory_space=pltpu.VMEM)] * 3,
        out_specs=pl.BlockSpec(memory_space=pltpu.VMEM),
        scratch_shapes=[pltpu.VMEM((RANK, RANK), F32)],
        name="solve",
    )(gram, gram_c, moments)


def coords():
    e = lax.axis_index("ep")
    t = lax.axis_index("tm")
    return e, t, t // N_X, t % N_X


def greet(tm_group, ep_group, layer_group):
    e, t, z, x = coords()
    barrier = pltpu.get_barrier_semaphore()
    count = 0
    if tm_group:

        def body(k, _):
            peer = lax.rem(t + k, N_TM)
            pl.semaphore_signal(barrier, inc=1, device_id=(e, peer), device_id_type=MESH)
            return 0

        lax.fori_loop(1, N_TM, body, 0)
        count += N_TM - 1
    if layer_group:

        def body(k, _):
            pe = lax.rem(e + k // N_X, N_EP)
            px = lax.rem(x + k % N_X, N_X)
            pl.semaphore_signal(barrier, inc=1, device_id=(pe, z * N_X + px), device_id_type=MESH)
            return 0

        lax.fori_loop(1, N_EP * N_X, body, 0)
        count += N_EP * N_X - 1
    elif ep_group:

        def body(k, _):
            peer = lax.rem(e + k, N_EP)
            pl.semaphore_signal(barrier, inc=1, device_id=(peer, t), device_id_type=MESH)
            return 0

        lax.fori_loop(1, N_EP, body, 0)
        count += N_EP - 1
    pl.semaphore_wait(barrier, count)


def send_tm(src_of, dst, send_sem, recv_sem):
    e, t, _, _ = coords()

    def body(k, _):
        peer = lax.rem(t + k, N_TM)
        pltpu.make_async_remote_copy(
            src_ref=src_of(peer),
            dst_ref=dst,
            send_sem=send_sem,
            recv_sem=recv_sem,
            device_id=(e, peer),
            device_id_type=MESH,
        ).start()
        return 0

    lax.fori_loop(1, N_TM, body, 0)


def send_ep(src_of, dst, send_sem, recv_sem):
    e, t, _, _ = coords()

    def body(k, _):
        peer = lax.rem(e + k, N_EP)
        pltpu.make_async_remote_copy(
            src_ref=src_of(peer),
            dst_ref=dst,
            send_sem=send_sem,
            recv_sem=recv_sem,
            device_id=(peer, t),
            device_id_type=MESH,
        ).start()
        return 0

    lax.fori_loop(1, N_EP, body, 0)


def send_layer(src, dst, send_sem, recv_sem):
    e, _, z, x = coords()

    def body(k, _):
        pe = lax.rem(e + k // N_X, N_EP)
        px = lax.rem(x + k % N_X, N_X)
        pltpu.make_async_remote_copy(
            src_ref=src,
            dst_ref=dst,
            send_sem=send_sem,
            recv_sem=recv_sem,
            device_id=(pe, z * N_X + px),
            device_id_type=MESH,
        ).start()
        return 0

    lax.fori_loop(1, N_EP * N_X, body, 0)


def settle(ref, sem):
    pltpu.make_async_copy(ref, ref, sem).wait()


def sum_slots(ref, slots, rows):
    parts = [ref[rows * s : rows * (s + 1), :] for s in range(slots)]
    while len(parts) > 1:
        parts = [parts[i] + parts[i + 1] for i in range(0, len(parts), 2)]
    return parts[0]


def scaled_rows(a_rows, chan):
    return jnp.concatenate([a_rows[i : i + 1, :] * chan for i in range(STEP_I)], axis=0)


def rows_at(index, size):
    return pl.ds(pl.multiple_of(index * size, size), size)


def model_chunk(a_rows, chan, wide, narrow):
    high, low = split2(scaled_rows(a_rows, chan))
    both = dot(high, wide)
    return (both[:, :J_BLK] + both[:, J_BLK:]) + dot(low, narrow)


def episode_kernel(
    first,
    obs_ref,
    miss_ref,
    a_ref,
    b_ref,
    chan_ref,
    filled_ref,
    m_ref,
    g_ref,
    x_buf,
    miss_buf,
    a_buf,
    b_buf,
    bt_buf,
    wide_buf,
    twice_buf,
    low_buf,
    gpart,
    grecv,
    gfull,
    part,
    mrecv,
    load_sem,
    send_sem,
    recv_sem,
):
    e, t, z, x = coords()
    load_x = pltpu.make_async_copy(obs_ref, x_buf, load_sem.at[0])
    load_m = pltpu.make_async_copy(miss_ref, miss_buf, load_sem.at[1])
    load_x.start()
    load_m.start()
    b_mine = rows_at(e, B_OWN)
    b_buf[b_mine, :] = b_ref[...]
    if first:
        a_mine = rows_at(t, A_OWN)
        a_buf[a_mine, :] = a_ref[...]
    greet(True, True, True)
    send_ep(lambda peer: b_buf.at[b_mine], b_buf.at[b_mine], send_sem.at[0], recv_sem.at[0])
    if first:
        send_tm(lambda peer: a_buf.at[a_mine], a_buf.at[a_mine], send_sem.at[1], recv_sem.at[1])
    others_b = b_buf.at[pl.ds(0, (N_EP - 1) * B_OWN)]
    settle(others_b, recv_sem.at[0])

    b = b_buf[...]
    bt = b.T
    bt_buf[...] = bt
    bt_high, bt_low = split2(bt)
    wide_buf[...] = jnp.concatenate([bt_high, bt_low], axis=1)
    b_high, b_low = split2(b)
    twice_buf[...] = jnp.concatenate([b_high, b_high], axis=0)
    low_buf[...] = b_low
    slab = N_X * PIECE
    gpart[...] = dot_high(bt_buf[rows_at(e, slab), :], b)
    g_slot = grecv.at[rows_at(t, PIECE)]
    send_tm(lambda peer: gpart.at[rows_at(peer % N_X, PIECE)], g_slot, send_sem.at[2], recv_sem.at[2])
    grecv[rows_at(t, PIECE), :] = gpart[rows_at(x, PIECE), :]
    if first:
        settle(a_buf.at[pl.ds(0, (N_TM - 1) * A_OWN)], recv_sem.at[1])
    load_x.wait()
    load_m.wait()

    def chunk(c, _):
        rows = rows_at(c, CHUNK)
        own = rows_at(c, STEP_I)
        chan = chan_ref[...]
        a_rows = a_buf[own, :] if first else a_ref[own, :]
        model = model_chunk(a_rows, chan, wide_buf[...], wide_buf[:, :J_BLK])
        filled = jnp.where(miss_buf[rows, :] == 1, model, x_buf[rows, :])
        x_buf[rows, :] = filled
        high, low = split2(filled)
        prod = dot(jnp.concatenate([high, low], axis=1), twice_buf[...]) + dot(high, low_buf[...])
        part[own, :] = jnp.sum(prod.reshape(STEP_I, WIDTH, RANK) * chan[None], axis=1)
        return 0

    lax.fori_loop(0, N_CHUNK // 2, chunk, 0)
    settle(grecv.at[pl.ds(0, (N_TM - 1) * PIECE)], recv_sem.at[2])
    g_mine = rows_at(e * N_X + x, PIECE)
    gfull[g_mine, :] = sum_slots(grecv, N_TM, PIECE)
    send_layer(gfull.at[g_mine], gfull.at[g_mine], send_sem.at[3], recv_sem.at[3])
    lax.fori_loop(N_CHUNK // 2, N_CHUNK, chunk, 0)
    save = pltpu.make_async_copy(x_buf, filled_ref, load_sem.at[2])
    save.start()
    m_slot = mrecv.at[rows_at(t, A_OWN)]
    send_tm(lambda peer: part.at[rows_at(peer, A_OWN)], m_slot, send_sem.at[4], recv_sem.at[4])
    mrecv[rows_at(t, A_OWN), :] = part[rows_at(t, A_OWN), :]
    settle(gfull.at[pl.ds(0, (N_EP * N_X - 1) * PIECE)], recv_sem.at[3])
    g_ref[...] = gfull[...]
    settle(mrecv.at[pl.ds(0, (N_TM - 1) * A_OWN)], recv_sem.at[4])
    m_ref[...] = sum_slots(mrecv, N_TM, A_OWN)
    save.wait()
    settle(others_b, send_sem.at[0])
    if first:
        settle(a_buf.at[pl.ds(0, (N_TM - 1) * A_OWN)], send_sem.at[1])
    settle(grecv.at[pl.ds(0, (N_TM - 1) * PIECE)], send_sem.at[2])
    settle(gfull.at[pl.ds(0, (N_EP * N_X - 1) * PIECE)], send_sem.at[3])
    settle(mrecv.at[pl.ds(0, (N_TM - 1) * A_OWN)], send_sem.at[4])


def episode_step(first, obs, miss, a, b_own, channel):
    vmem = pl.BlockSpec(memory_space=pltpu.VMEM)
    anywhere = pl.BlockSpec(memory_space=pl.ANY)
    return pl.pallas_call(
        functools.partial(episode_kernel, first),
        out_shape=(
            jax.ShapeDtypeStruct((ROWS, J_BLK), F32),
            jax.ShapeDtypeStruct((A_OWN, RANK), F32),
            jax.ShapeDtypeStruct((RANK, RANK), F32),
        ),
        in_specs=[anywhere, anywhere, vmem, vmem, vmem],
        out_specs=(anywhere, vmem, vmem),
        scratch_shapes=[
            pltpu.VMEM((ROWS, J_BLK), F32),
            pltpu.VMEM((ROWS, J_BLK), jnp.int32),
            pltpu.VMEM((I_BLK, RANK), F32),
            pltpu.VMEM((J_BLK, RANK), F32),
            pltpu.VMEM((RANK, J_BLK), F32),
            pltpu.VMEM((RANK, 2 * J_BLK), BF16),
            pltpu.VMEM((2 * J_BLK, RANK), BF16),
            pltpu.VMEM((J_BLK, RANK), BF16),
            pltpu.VMEM((N_X * PIECE, RANK), F32),
            pltpu.VMEM((N_TM * PIECE, RANK), F32),
            pltpu.VMEM((RANK, RANK), F32),
            pltpu.VMEM((I_BLK, RANK), F32),
            pltpu.VMEM((I_BLK, RANK), F32),
            pltpu.SemaphoreType.DMA((3,)),
            pltpu.SemaphoreType.DMA((5,)),
            pltpu.SemaphoreType.DMA((5,)),
        ],
        compiler_params=pltpu.CompilerParams(
            collective_id=0 if first else 1,
            has_side_effects=True,
            vmem_limit_bytes=VMEM_LIMIT,
        ),
        name="episode_first" if first else "episode",
    )(obs, miss, a, b_own, channel)


def time_kernel(
    filled_ref,
    a_ref,
    chan_ref,
    ablk_ref,
    m_ref,
    g_ref,
    x_buf,
    a_buf,
    at_buf,
    gpart,
    grecv,
    gfull,
    part,
    mrecv,
    load_sem,
    send_sem,
    recv_sem,
):
    e, t, z, x = coords()
    load_x = pltpu.make_async_copy(filled_ref, x_buf, load_sem.at[0])
    load_x.start()
    a_mine = rows_at(t, A_OWN)
    a_buf[a_mine, :] = a_ref[...]
    greet(True, True, True)
    send_tm(lambda peer: a_buf.at[a_mine], a_buf.at[a_mine], send_sem.at[0], recv_sem.at[0])
    others_a = a_buf.at[pl.ds(0, (N_TM - 1) * A_OWN)]
    settle(others_a, recv_sem.at[0])

    a = a_buf[...]
    ablk_ref[...] = a
    at_buf[...] = a.T
    gpart[...] = dot_high(at_buf[rows_at(x, N_EP * PIECE), :], a)
    g_slot = grecv.at[rows_at(e, PIECE)]
    send_ep(lambda peer: gpart.at[rows_at(peer, PIECE)], g_slot, send_sem.at[1], recv_sem.at[1])
    grecv[rows_at(e, PIECE), :] = gpart[rows_at(e, PIECE), :]
    load_x.wait()
    part[...] = jnp.zeros_like(part)

    def chunk(c, _):
        high, low = split2(x_buf[rows_at(c, CHUNK), :])
        ac_high, ac_low = split2(scaled_rows(a_buf[rows_at(c, STEP_I), :], chan_ref[...]))
        high_t = high.T
        both = dot(jnp.concatenate([high_t, low.T], axis=0), ac_high)
        part[...] += (both[:J_BLK] + both[J_BLK:]) + dot(high_t, ac_low)
        return 0

    lax.fori_loop(0, N_CHUNK // 2, chunk, 0)
    settle(grecv.at[pl.ds(0, (N_EP - 1) * PIECE)], recv_sem.at[1])
    g_mine = rows_at(x * N_EP + e, PIECE)
    gfull[g_mine, :] = sum_slots(grecv, N_EP, PIECE)
    send_layer(gfull.at[g_mine], gfull.at[g_mine], send_sem.at[2], recv_sem.at[2])
    lax.fori_loop(N_CHUNK // 2, N_CHUNK, chunk, 0)
    m_slot = mrecv.at[rows_at(e, B_OWN)]
    send_ep(lambda peer: part.at[rows_at(peer, B_OWN)], m_slot, send_sem.at[3], recv_sem.at[3])
    mrecv[rows_at(e, B_OWN), :] = part[rows_at(e, B_OWN), :]
    settle(gfull.at[pl.ds(0, (N_EP * N_X - 1) * PIECE)], recv_sem.at[2])
    g_ref[...] = gfull[...]
    settle(mrecv.at[pl.ds(0, (N_EP - 1) * B_OWN)], recv_sem.at[3])
    m_ref[...] = sum_slots(mrecv, N_EP, B_OWN)
    settle(others_a, send_sem.at[0])
    settle(grecv.at[pl.ds(0, (N_EP - 1) * PIECE)], send_sem.at[1])
    settle(gfull.at[pl.ds(0, (N_EP * N_X - 1) * PIECE)], send_sem.at[2])
    settle(mrecv.at[pl.ds(0, (N_EP - 1) * B_OWN)], send_sem.at[3])


def time_step(filled, a_own, channel):
    vmem = pl.BlockSpec(memory_space=pltpu.VMEM)
    anywhere = pl.BlockSpec(memory_space=pl.ANY)
    return pl.pallas_call(
        time_kernel,
        out_shape=(
            jax.ShapeDtypeStruct((I_BLK, RANK), F32),
            jax.ShapeDtypeStruct((B_OWN, RANK), F32),
            jax.ShapeDtypeStruct((RANK, RANK), F32),
        ),
        in_specs=[anywhere, vmem, vmem],
        out_specs=(vmem, vmem, vmem),
        scratch_shapes=[
            pltpu.VMEM((ROWS, J_BLK), F32),
            pltpu.VMEM((I_BLK, RANK), F32),
            pltpu.VMEM((RANK, I_BLK), F32),
            pltpu.VMEM((N_EP * PIECE, RANK), F32),
            pltpu.VMEM((N_EP * PIECE, RANK), F32),
            pltpu.VMEM((RANK, RANK), F32),
            pltpu.VMEM((J_BLK, RANK), F32),
            pltpu.VMEM((J_BLK, RANK), F32),
            pltpu.SemaphoreType.DMA((1,)),
            pltpu.SemaphoreType.DMA((4,)),
            pltpu.SemaphoreType.DMA((4,)),
        ],
        compiler_params=pltpu.CompilerParams(
            collective_id=2, has_side_effects=True, vmem_limit_bytes=VMEM_LIMIT
        ),
        name="time",
    )(filled, a_own, channel)


def gather_kernel(b_ref, out_ref, b_buf, send_sem, recv_sem):
    e = lax.axis_index("ep")
    b_mine = rows_at(e, B_OWN)
    b_buf[b_mine, :] = b_ref[...]
    greet(False, True, False)
    send_ep(lambda peer: b_buf.at[b_mine], b_buf.at[b_mine], send_sem.at[0], recv_sem.at[0])
    others_b = b_buf.at[pl.ds(0, (N_EP - 1) * B_OWN)]
    settle(others_b, recv_sem.at[0])
    out_ref[...] = b_buf[...]
    settle(others_b, send_sem.at[0])


def gather_time(b_own):
    return pl.pallas_call(
        gather_kernel,
        out_shape=jax.ShapeDtypeStruct((J_BLK, RANK), F32),
        in_specs=[pl.BlockSpec(memory_space=pltpu.VMEM)],
        out_specs=pl.BlockSpec(memory_space=pltpu.VMEM),
        scratch_shapes=[
            pltpu.VMEM((J_BLK, RANK), F32),
            pltpu.SemaphoreType.DMA((1,)),
            pltpu.SemaphoreType.DMA((1,)),
        ],
        compiler_params=pltpu.CompilerParams(collective_id=3, has_side_effects=True),
        name="gather_time",
    )(b_own)


GRID = 8


def complete_kernel(obs_ref, miss_ref, a_ref, b_ref, chan_ref, out_ref, wide_buf):
    @pl.when(pl.program_id(0) == 0)
    def _():
        high, low = split2(b_ref[...].T)
        wide_buf[...] = jnp.concatenate([high, low], axis=1)

    chan = chan_ref[...]

    def chunk(c, _):
        rows = rows_at(c, CHUNK)
        model = model_chunk(a_ref[rows_at(c, STEP_I), :], chan, wide_buf[...], wide_buf[:, :J_BLK])
        out_ref[rows, :] = jnp.where(miss_ref[rows, :] == 1, model, obs_ref[rows, :])
        return 0

    lax.fori_loop(0, N_CHUNK // GRID, chunk, 0)


def complete(obs, miss, a_block, b_block, channel):
    rows = ROWS // GRID
    return pl.pallas_call(
        complete_kernel,
        grid=(GRID,),
        out_shape=jax.ShapeDtypeStruct((ROWS, J_BLK), F32),
        in_specs=[
            pl.BlockSpec((rows, J_BLK), lambda i: (i, 0)),
            pl.BlockSpec((rows, J_BLK), lambda i: (i, 0)),
            pl.BlockSpec((I_BLK // GRID, RANK), lambda i: (i, 0)),
            pl.BlockSpec((J_BLK, RANK), lambda i: (0, 0)),
            pl.BlockSpec((WIDTH, RANK), lambda i: (0, 0)),
        ],
        out_specs=pl.BlockSpec((rows, J_BLK), lambda i: (i, 0)),
        scratch_shapes=[pltpu.VMEM((RANK, 2 * J_BLK), BF16)],
        compiler_params=pltpu.CompilerParams(vmem_limit_bytes=VMEM_LIMIT),
        name="complete",
    )(obs, miss, a_block, b_block, channel)


def on_device(observed, missing, episode_init, time_init, channel):
    obs = observed.transpose(0, 2, 1).reshape(ROWS, J_BLK)
    miss = missing.transpose(0, 2, 1).reshape(ROWS, J_BLK)
    gram_c = lax.dot_general(
        channel, channel, (((0,), (0,)), ((), ())), precision=HIGH, preferred_element_type=F32
    )
    a = episode_init
    b_own = time_init
    for sweep in range(SWEEPS):
        filled, m_own, gram = episode_step(sweep == 0, obs, miss, a, b_own, channel)
        a_own = solve_rows(gram, gram_c, m_own)
        a, m_own, gram = time_step(filled, a_own, channel)
        b_own = solve_rows(gram, gram_c, m_own)
    b = gather_time(b_own)
    out = complete(obs, miss, a, b, channel)
    return out.reshape(I_BLK, WIDTH, J_BLK).transpose(0, 2, 1)


def solution(mesh):
    in_specs = (
        P("ep", "tm", None),
        P("ep", "tm", None),
        P(("ep", "tm"), None),
        P(("tm", "ep"), None),
        P(),
    )
    return jax.shard_map(
        on_device, mesh=mesh, in_specs=in_specs, out_specs=P("ep", "tm", None), check_vma=False
    )
```

time: 1340 us -> 206 us (0.15)
  waiting for transfers between devices: 819 us -> 0 us
  other arithmetic: 225 us -> 0 us
  Pallas kernels: 0 us -> 204 us
  blocking collectives: 164 us -> 0 us
  matrix products: 64.3 us -> 1.95 us
  local copies, waits for them, and re-layouts: 38 us -> 0 us
  between operations: 21.1 us -> 0.04 us
    psum x4 -> x0, waiting for transfers between devices: 819 us -> none  [shard_gram(): return lax.psum(gram_rows(own_rows), ('ep', 'tm'))]
    another operation x36 -> x0, other arithmetic: 217 us -> none  [the longest x27 138 us: system_factor(): return jnp.linalg.cholesky(system)]
    pallas_call x0 -> x10, Pallas kernels: none -> 204 us  [the longest x2 73.9 us: episode_step(): pl.pallas_call(functools.partial(episode_kernel, first), out_shape=(jax.S...]
    all_gather x6 -> x0, blocking collectives: 164 us -> none  [the longest x3 118 us: gather_episode(): return lax.all_gather(rows, 'tm', axis=0, tiled=True)]
    dot_general x12 -> x1, matrix products: 51.3 us -> 1.95 us  [on_device(): lax.dot_general(channel, channel, (((0,), (0,)), ((), ())), precision=HIG...]
    another operation x37 -> x0, local copies, waits for them, and re-layouts: 16.4 us -> none  [the longest x29 16.3 us: solve_rows(): return jax.scipy.linalg.cho_solve((lower, True), moments.T).T]
  transfers between devices with their start and end apart: 8 -> 0, of which waited for: 4 -> 0; matrix products, arithmetic and copies ran while one was open for 22% -> 0% of each run, Pallas kernels for 0% -> 0%
where the time goes in v1:
time: 206 us
  Pallas kernels  204 us (99%)
    pallas_call x2, Pallas kernels, episode_step(): pl.pallas_call(functools.partial(episode_kernel, first), out_shape=(jax.S...  73.9 us
    pallas_call x2, Pallas kernels, time_step(): pl.pallas_call(time_kernel, out_shape=(jax.ShapeDtypeStruct((I_BLK, RANK)...  66.9 us
    pallas_call x4, Pallas kernels, solve_rows(): pl.pallas_call(solve_kernel, out_shape=jax.ShapeDtypeStruct(moments.shape...  44.2 us
    pallas_call x1, Pallas kernels, complete(): pl.pallas_call(complete_kernel, grid=(GRID,), out_shape=jax.ShapeDtypeStr...  11.4 us
    pallas_call x1, Pallas kernels, gather_time(): pl.pallas_call(gather_kernel, out_shape=jax.ShapeDtypeStruct((J_BLK, RANK...  7.14 us

profile of v1, /device:TPU:1, one launch (start us, length us, event | category | flops | bytes accessed | tf_op | source)
XLA Modules:
  0.0 205.5 jit_solution(16839651868484472688)
XLA Ops:
  0.0 1.9 fusion.gc_ref
  2.0 42.1 %episode_first.1 = (f32[8192,128]{1,0:T(8,128)}, f32[8,256]{1,0:T(8,128)}, f32[256,256]{1,0:T(8,128)}) custom-call(f32[8192,128]{1,0:T(8,128)} %bitcast.11, s32[8192,128]{1,0:T(8,128)} %bitcast.14, f32[8,256]{1,0:T(8,128)} %a_ref.1, f32[16,256]{1,0:T(8,128)} %b_ref.1, f32[32,256]{1,0:T(8,128)} %chan_ref.9), custom_call_target="tpu_custom_call" | custom-call | tf_op jit(solution)/shard_map/episode_first/pallas_call | solution.py:386
  44.1 11.0 %solve.4.a_ref = f32[8,256]{1,0:T(8,128)} custom-call(f32[256,256]{1,0:T(8,128)} %get-tuple-element.18.g_ref, f32[256,256]{1,0:T(8,128)} %fusion.gc_ref, f32[8,256]{1,0:T(8,128)} %get-tuple-element.19.m_ref), custom_call_target="tpu_custom_call" | custom-call | tf_op jit(solution)/shard_map/solve/pallas_call | solution.py:153
  55.1 32.9 %time.2 = (f32[256,256]{1,0:T(8,128)}, f32[16,256]{1,0:T(8,128)}, f32[256,256]{1,0:T(8,128)}) custom-call(f32[8192,128]{1,0:T(8,128)} %get-tuple-element.17.filled_ref, f32[8,256]{1,0:T(8,128)} %solve.4.a_ref, f32[32,256]{1,0:T(8,128)} %chan_ref.9), custom_call_target="tpu_custom_call" | custom-call | tf_op jit(solution)/shard_map/time/pallas_call | solution.py:491
  88.0 11.1 %solve.5.b_ref = f32[16,256]{1,0:T(8,128)} custom-call(f32[256,256]{1,0:T(8,128)} %get-tuple-element.21.g_ref, f32[256,256]{1,0:T(8,128)} %fusion.gc_ref, f32[16,256]{1,0:T(8,128)} %get-tuple-element.22.m_ref), custom_call_target="tpu_custom_call" | custom-call | tf_op jit(solution)/shard_map/solve/pallas_call | solution.py:153
  99.1 31.8 %episode.1 = (f32[8192,128]{1,0:T(8,128)}, f32[8,256]{1,0:T(8,128)}, f32[256,256]{1,0:T(8,128)}) custom-call(f32[8192,128]{1,0:T(8,128)} %bitcast.12, s32[8192,128]{1,0:T(8,128)} %bitcast.15, f32[256,256]{1,0:T(8,128)} %get-tuple-element.20.a_ref, f32[16,256]{1,0:T(8,128)} %solve.5.b_ref, f32[32,256]{1,0:T(8,128)} %chan_ref.9), custom_call_target="tpu_custom_call" | custom-call | tf_op jit(solution)/shard_map/episode/pallas_call | solution.py:386
  130.9 11.0 %solve.6.a_ref = f32[8,256]{1,0:T(8,128)} custom-call(f32[256,256]{1,0:T(8,128)} %get-tuple-element.24.g_ref, f32[256,256]{1,0:T(8,128)} %fusion.gc_ref, f32[8,256]{1,0:T(8,128)} %get-tuple-element.25.m_ref), custom_call_target="tpu_custom_call" | custom-call | tf_op jit(solution)/shard_map/solve/pallas_call | solution.py:153
  141.9 33.9 %time.3 = (f32[256,256]{1,0:T(8,128)}, f32[16,256]{1,0:T(8,128)}, f32[256,256]{1,0:T(8,128)}) custom-call(f32[8192,128]{1,0:T(8,128)} %get-tuple-element.23.filled_ref, f32[8,256]{1,0:T(8,128)} %solve.6.a_ref, f32[32,256]{1,0:T(8,128)} %chan_ref.9), custom_call_target="tpu_custom_call" | custom-call | tf_op jit(solution)/shard_map/time/pallas_call | solution.py:491
  175.9 11.1 %solve.7.b_ref = f32[16,256]{1,0:T(8,128)} custom-call(f32[256,256]{1,0:T(8,128)} %get-tuple-element.27.g_ref, f32[256,256]{1,0:T(8,128)} %fusion.gc_ref, f32[16,256]{1,0:T(8,128)} %get-tuple-element.28.m_ref), custom_call_target="tpu_custom_call" | custom-call | tf_op jit(solution)/shard_map/solve/pallas_call | solution.py:153
  186.9 7.1 %gather_time.1.b_ref = f32[128,256]{1,0:T(8,128)} custom-call(f32[16,256]{1,0:T(8,128)} %solve.7.b_ref), custom_call_target="tpu_custom_call" | custom-call | tf_op jit(solution)/shard_map/gather_time/pallas_call | solution.py:533
  194.1 11.4 %complete.1 = f32[8192,128]{1,0:T(8,128)} custom-call(f32[8192,128]{1,0:T(8,128)} %bitcast.13, s32[8192,128]{1,0:T(8,128)} %bitcast.16, f32[256,256]{1,0:T(8,128)} %get-tuple-element.26.a_ref, f32[128,256]{1,0:T(8,128)} %gather_time.1.b_ref, f32[32,256]{1,0:T(8,128)} %chan_ref.9), custom_call_target="tpu_custom_call" | custom-call | tf_op jit(solution)/shard_map/complete/pallas_call | solution.py:570

commit v2 on v0

v2 whole, which is shorter than its diff:
```python
import jax
import jax.numpy as jnp
from jax import lax
from jax.experimental import pallas as pl
from jax.experimental.pallas import tpu as pltpu
from jax.sharding import PartitionSpec as P

SWEEPS = 2
RIDGE = 1.0
HIGH = lax.Precision.HIGHEST
F32 = jnp.float32
BF16 = jnp.bfloat16
MESH = pl.DeviceIdType.MESH

RANK = 256
WIDTH = 32
N_EP = 8
N_TM = 32
N_X = 4
I_BLK = 256
J_BLK = 128
ROWS = I_BLK * WIDTH
GROUP = 8
N_GROUP = WIDTH // GROUP
G_ROWS = GROUP * I_BLK
A_OWN = 8
B_OWN = 16
PIECE = 8
VMEM_LIMIT = 56 * 1024 * 1024


def dot(left, right):
    return lax.dot_general(
        left, right, (((1,), (0,)), ((), ())), preferred_element_type=F32
    )


def dot_high(left, right):
    return lax.dot_general(
        left, right, (((1,), (0,)), ((), ())), precision=HIGH, preferred_element_type=F32
    )


def split2(x):
    high = x.astype(BF16)
    return high, (x - high.astype(F32)).astype(BF16)


def split3(x):
    high = x.astype(BF16)
    rest = x - high.astype(F32)
    mid = rest.astype(BF16)
    return high, mid, (rest - mid.astype(F32)).astype(BF16)


def dot_packed(left, right):
    a0, a1, a2 = split3(left)
    b0, b1, b2 = split3(right)
    lhs = jnp.concatenate([a0, a0, a1, a0, a2, a1], axis=1)
    rhs = jnp.concatenate([b0, b1, b0, b2, b0, b1], axis=0)
    return dot(lhs, rhs)


def invert8(cols):
    row = lax.broadcasted_iota(jnp.int32, (8, 128), 0)
    for s in range(8):
        here = row == s
        at_s = [jnp.broadcast_to(cols[q][s : s + 1, :], (8, 128)) for q in range(8)]
        inv = 1.0 / at_s[s]
        pivot = cols[s]
        fresh = []
        for q in range(8):
            if q == s:
                fresh.append(jnp.where(here, inv, -pivot * inv))
            else:
                scaled = at_s[q] * inv
                fresh.append(jnp.where(here, scaled, cols[q] - pivot * scaled))
        cols = fresh
    return cols


def spread_row(x, m):
    return jnp.broadcast_to(x[m : m + 1, :], (8, 128))


def eliminate_panel(ref, r0, depth, n):
    tiles = n // 128
    groups = depth // 8
    lane = lax.broadcasted_iota(jnp.int32, (8, 128), 1)
    row = lax.broadcasted_iota(jnp.int32, (8, 128), 0)
    x = [
        [ref[r0 + 8 * v : r0 + 8 * v + 8, 128 * t : 128 * t + 128] for t in range(tiles)]
        for v in range(groups)
    ]
    for g in range(groups):
        t_piv, l0 = divmod(r0 + 8 * g, 128)

        def column(block, q):
            return jnp.broadcast_to(block[:, l0 + q : l0 + q + 1], (8, 128))

        inv = invert8([column(x[g][t_piv], q) for q in range(8)])
        inside = (lane >= l0) & (lane < l0 + 8)
        unit = jnp.where(lane - l0 == row, 1.0, 0.0)
        fresh = []
        for t in range(tiles):
            old = x[g][t]
            if t == t_piv:
                old = jnp.where(inside, unit, old)
            y = [inv[m] * spread_row(old, m) for m in range(8)]
            fresh.append(((y[0] + y[1]) + (y[2] + y[3])) + ((y[4] + y[5]) + (y[6] + y[7])))
        for v in range(groups):
            if v == g:
                continue
            cols = [column(x[v][t_piv], m) for m in range(8)]
            for t in range(tiles):
                old = x[v][t]
                if t == t_piv:
                    old = jnp.where(inside, 0.0, old)
                y = [cols[m] * spread_row(fresh[t], m) for m in range(8)]
                x[v][t] = old - (
                    ((y[0] + y[1]) + (y[2] + y[3])) + ((y[4] + y[5]) + (y[6] + y[7]))
                )
        x[g] = fresh
    for v in range(groups):
        for t in range(tiles):
            ref[r0 + 8 * v : r0 + 8 * v + 8, 128 * t : 128 * t + 128] = x[v][t]


def invert_in_place(ref, n, depth):
    for k in range(n // depth):
        r0 = k * depth
        eliminate_panel(ref, r0, depth, n)
        panel = ref[r0 : r0 + depth, :]
        lane = lax.broadcasted_iota(jnp.int32, (1, n), 1)
        inside = (lane >= r0) & (lane < r0 + depth)
        for lo, hi in ((0, r0), (r0 + depth, n)):
            if hi > lo:
                cols = ref[lo:hi, r0 : r0 + depth]
                ref[lo:hi, :] = jnp.where(inside, 0.0, ref[lo:hi, :]) - dot_packed(cols, panel)


def coords():
    e = lax.axis_index("ep")
    t = lax.axis_index("tm")
    return e, t, t // N_X, t % N_X


def greet():
    e, t, z, x = coords()
    barrier = pltpu.get_barrier_semaphore()

    def along_tm(k, _):
        peer = lax.rem(t + k, N_TM)
        pl.semaphore_signal(barrier, inc=1, device_id=(e, peer), device_id_type=MESH)
        return 0

    def in_layer(k, _):
        pe = lax.rem(e + k // N_X, N_EP)
        px = lax.rem(x + k % N_X, N_X)
        pl.semaphore_signal(barrier, inc=1, device_id=(pe, z * N_X + px), device_id_type=MESH)
        return 0

    lax.fori_loop(1, N_TM, along_tm, 0)
    lax.fori_loop(N_X, N_EP * N_X, in_layer, 0)
    pl.semaphore_wait(barrier, N_TM - 1 + (N_EP - 1) * N_X)


def send_tm(src_of, dst, send_sem, recv_sem):
    e, t, _, _ = coords()

    def body(k, _):
        peer = lax.rem(t + k, N_TM)
        pltpu.make_async_remote_copy(
            src_ref=src_of(peer),
            dst_ref=dst,
            send_sem=send_sem,
            recv_sem=recv_sem,
            device_id=(e, peer),
            device_id_type=MESH,
        ).start()
        return 0

    lax.fori_loop(1, N_TM, body, 0)


def send_ep(src_of, dst, send_sem, recv_sem):
    e, t, _, _ = coords()

    def body(k, _):
        peer = lax.rem(e + k, N_EP)
        pltpu.make_async_remote_copy(
            src_ref=src_of(peer),
            dst_ref=dst,
            send_sem=send_sem,
            recv_sem=recv_sem,
            device_id=(peer, t),
            device_id_type=MESH,
        ).start()
        return 0

    lax.fori_loop(1, N_EP, body, 0)


def send_layer(src, dst, send_sem, recv_sem):
    e, _, z, x = coords()

    def body(k, _):
        pe = lax.rem(e + k // N_X, N_EP)
        px = lax.rem(x + k % N_X, N_X)
        pltpu.make_async_remote_copy(
            src_ref=src,
            dst_ref=dst,
            send_sem=send_sem,
            recv_sem=recv_sem,
            device_id=(pe, z * N_X + px),
            device_id_type=MESH,
        ).start()
        return 0

    lax.fori_loop(1, N_EP * N_X, body, 0)


def settle(ref, sem):
    pltpu.make_async_copy(ref, ref, sem).wait()


def sum_slots(ref, slots, rows):
    parts = [ref[rows * s : rows * (s + 1), :] for s in range(slots)]
    while len(parts) > 1:
        parts = [parts[i] + parts[i + 1] for i in range(0, len(parts), 2)]
    return parts[0]


def rows_at(index, size):
    return pl.ds(pl.multiple_of(index * size, size), size)


def dot_t(left, right):
    return lax.dot_general(
        left, right, (((1,), (1,)), ((), ())), preferred_element_type=F32
    )


def basis_pair(b, chan_ref, k):
    return split2(jnp.concatenate([b * chan_ref[pl.ds(k + d, 1), :] for d in range(2)], axis=0))


def model_pair(acat, high, low):
    return dot_t(acat, jnp.concatenate([high, high, low], axis=1))


def pack_left(x):
    high, low = split2(x)
    return jnp.concatenate([high, low, high], axis=1)


def fit_kernel(
    obs_ref,
    miss_ref,
    a_ref,
    b_ref,
    chan_ref,
    w_ref,
    aout_ref,
    bout_ref,
    w_buf,
    miss_buf,
    xh_buf,
    xl_buf,
    a_buf,
    b_buf,
    acat,
    spread,
    gram_c,
    s_buf,
    bt_buf,
    gb_part,
    gb_recv,
    gb_full,
    me_part,
    me_recv,
    at_buf,
    ga_part,
    ga_recv,
    ga_full,
    mt_part,
    mt_acc,
    mt_recv,
    load_sem,
    save_sem,
    send_sem,
    recv_sem,
):
    e, t, z, x = coords()
    for g in range(N_GROUP):
        for q in range(GROUP):
            k = g * GROUP + q
            to = pl.ds(k * I_BLK, I_BLK)
            pltpu.make_async_copy(obs_ref.at[:, k, :], w_buf.at[to], load_sem.at[g]).start()
            pltpu.make_async_copy(miss_ref.at[:, k, :], miss_buf.at[to], load_sem.at[N_GROUP + g]).start()
    a_mine = rows_at(t, A_OWN)
    b_mine = rows_at(e, B_OWN)
    a_buf[a_mine, :] = a_ref[...]
    b_buf[b_mine, :] = b_ref[...]
    others_a = a_buf.at[pl.ds(0, (N_TM - 1) * A_OWN)]
    others_b = b_buf.at[pl.ds(0, (N_EP - 1) * B_OWN)]
    others_gb = gb_recv.at[pl.ds(0, (N_TM - 1) * PIECE)]
    others_gb_full = gb_full.at[pl.ds(0, (N_EP * N_X - 1) * PIECE)]
    others_me = me_recv.at[pl.ds(0, (N_TM - 1) * A_OWN)]
    others_ga = ga_recv.at[pl.ds(0, (N_EP - 1) * PIECE)]
    others_ga_full = ga_full.at[pl.ds(0, (N_EP * N_X - 1) * PIECE)]
    others_mt = mt_recv.at[pl.ds(0, (N_EP - 1) * B_OWN)]

    def send_b():
        send_ep(lambda peer: b_buf.at[b_mine], b_buf.at[b_mine], send_sem.at[0], recv_sem.at[0])

    def send_a():
        send_tm(lambda peer: a_buf.at[a_mine], a_buf.at[a_mine], send_sem.at[1], recv_sem.at[1])

    greet()
    send_b()
    send_a()

    chan_t = chan_ref[...].T
    gram_c[...] = dot_high(chan_t, chan_ref[...])
    for g in range(N_GROUP):
        spread[g] = chan_t[:, g * GROUP : (g + 1) * GROUP]

    def mask_group(g, _):
        rows = rows_at(g, G_ROWS)
        settle(w_buf.at[rows], load_sem.at[g])
        settle(miss_buf.at[rows], load_sem.at[N_GROUP + g])

        def mask_part(q, _):
            part = rows_at(g * GROUP + q, I_BLK)
            w_buf[part, :] = jnp.where(miss_buf[part, :] == 1, jnp.nan, w_buf[part, :])
            return 0

        lax.fori_loop(0, GROUP, mask_part, 0)
        return 0

    lax.fori_loop(0, N_GROUP, mask_group, 0)
    save = pltpu.make_async_copy(w_buf, w_ref, save_sem.at[0])
    save.start()
    settle(others_a, recv_sem.at[1])
    settle(others_a, send_sem.at[1])

    def sweep(s, _):
        acat[...] = pack_left(a_buf[...])
        me_part[...] = jnp.zeros_like(me_part)
        settle(others_b, recv_sem.at[0])
        settle(others_b, send_sem.at[0])
        b = b_buf[...]
        bt_buf[...] = b.T
        gb_part[...] = dot_high(bt_buf[rows_at(e, N_X * PIECE), :], b)
        gb_slot = gb_recv.at[rows_at(t, PIECE)]
        send_tm(
            lambda peer: gb_part.at[rows_at(peer % N_X, PIECE)], gb_slot, send_sem.at[2], recv_sem.at[2]
        )
        gb_recv[rows_at(t, PIECE), :] = gb_part[rows_at(x, PIECE), :]

        def episode_group(g, _):
            for p in range(0, GROUP, 2):
                k = g * GROUP + p
                b_high, b_low = basis_pair(b_buf[...], chan_ref, k)
                model = model_pair(acat[...], b_high, b_low)
                highs, lows = [], []
                for d in range(2):
                    rows = rows_at(k + d, I_BLK)
                    w = w_buf[rows, :]
                    filled = jnp.where(w != w, model[:, d * J_BLK : (d + 1) * J_BLK], w)
                    high, low = split2(filled)
                    xh_buf[rows, :] = high
                    xl_buf[rows, :] = low
                    highs.append(high)
                    lows.append(low)
                high = jnp.concatenate(highs, axis=1)
                low = jnp.concatenate(lows, axis=1)
                me_part[...] += dot(
                    jnp.concatenate([high, low, high], axis=1),
                    jnp.concatenate([b_high, b_high, b_low], axis=0),
                )
            return 0

        lax.fori_loop(0, N_GROUP, episode_group, 0)
        me_slot = me_recv.at[rows_at(t, A_OWN)]
        send_tm(lambda peer: me_part.at[rows_at(peer, A_OWN)], me_slot, send_sem.at[4], recv_sem.at[4])
        me_recv[rows_at(t, A_OWN), :] = me_part[rows_at(t, A_OWN), :]
        settle(others_gb, recv_sem.at[2])
        gb_mine = rows_at(e * N_X + x, PIECE)
        gb_full[gb_mine, :] = sum_slots(gb_recv, N_TM, PIECE)
        send_layer(gb_full.at[gb_mine], gb_full.at[gb_mine], send_sem.at[3], recv_sem.at[3])
        settle(others_gb_full, recv_sem.at[3])
        form_system(s_buf, gb_full, gram_c)
        invert_in_place(s_buf, RANK, 32)
        settle(others_me, recv_sem.at[4])
        a_buf[a_mine, :] = dot_high(sum_slots(me_recv, N_TM, A_OWN), s_buf[...])
        send_a()
        settle(others_gb, send_sem.at[2])
        settle(others_gb_full, send_sem.at[3])
        settle(others_me, send_sem.at[4])

        settle(others_a, recv_sem.at[1])
        settle(others_a, send_sem.at[1])
        a = a_buf[...]
        at = a.T
        at_buf[...] = at
        ga_part[...] = dot_high(at_buf[rows_at(x, N_EP * PIECE), :], a)
        ga_slot = ga_recv.at[rows_at(e, PIECE)]
        send_ep(lambda peer: ga_part.at[rows_at(peer, PIECE)], ga_slot, send_sem.at[5], recv_sem.at[5])
        ga_recv[rows_at(e, PIECE), :] = ga_part[rows_at(e, PIECE), :]
        acat[...] = pack_left(at_buf[...])
        mt_acc[...] = jnp.zeros_like(mt_acc)

        def time_group(g, _):
            for p in range(0, GROUP, 2):
                k = g * GROUP + p
                high = jnp.concatenate([xh_buf[rows_at(k + d, I_BLK), :] for d in range(2)], axis=1)
                low = jnp.concatenate([xl_buf[rows_at(k + d, I_BLK), :] for d in range(2)], axis=1)
                prod = dot(acat[...], jnp.concatenate([high, high, low], axis=0))
                terms = [
                    jnp.broadcast_to(spread[g, :, p + d : p + d + 1], (RANK, J_BLK))
                    * prod[:, d * J_BLK : (d + 1) * J_BLK]
                    for d in range(2)
                ]
                mt_acc[...] += terms[0] + terms[1]
            return 0

        lax.fori_loop(0, N_GROUP, time_group, 0)
        mt_part[...] = mt_acc[...].T
        mt_slot = mt_recv.at[rows_at(e, B_OWN)]
        send_ep(lambda peer: mt_part.at[rows_at(peer, B_OWN)], mt_slot, send_sem.at[7], recv_sem.at[7])
        mt_recv[rows_at(e, B_OWN), :] = mt_part[rows_at(e, B_OWN), :]
        settle(others_ga, recv_sem.at[5])
        ga_mine = rows_at(x * N_EP + e, PIECE)
        ga_full[ga_mine, :] = sum_slots(ga_recv, N_EP, PIECE)
        send_layer(ga_full.at[ga_mine], ga_full.at[ga_mine], send_sem.at[6], recv_sem.at[6])
        settle(others_ga_full, recv_sem.at[6])
        form_system(s_buf, ga_full, gram_c)
        invert_in_place(s_buf, RANK, 32)
        settle(others_mt, recv_sem.at[7])
        b_buf[b_mine, :] = dot_high(sum_slots(mt_recv, N_EP, B_OWN), s_buf[...])
        send_b()
        settle(others_ga, send_sem.at[5])
        settle(others_ga_full, send_sem.at[6])
        settle(others_mt, send_sem.at[7])
        return 0

    lax.fori_loop(0, SWEEPS, sweep, 0)
    aout_ref[...] = a_buf[...]
    settle(others_b, recv_sem.at[0])
    settle(others_b, send_sem.at[0])
    bout_ref[...] = b_buf[...]
    save.wait()


def form_system(s_ref, gram_ref, gram_c):
    eye = lax.broadcasted_iota(jnp.int32, (RANK, RANK), 0) == lax.broadcasted_iota(
        jnp.int32, (RANK, RANK), 1
    )
    s_ref[...] = gram_ref[...] * gram_c[...] + jnp.where(eye, RIDGE, 0.0)


def fit(obs, miss, a_own, b_own, channel):
    vmem = pl.BlockSpec(memory_space=pltpu.VMEM)
    anywhere = pl.BlockSpec(memory_space=pl.ANY)

    def f32(*shape):
        return pltpu.VMEM(shape, F32)

    return pl.pallas_call(
        fit_kernel,
        out_shape=(
            jax.ShapeDtypeStruct((ROWS, J_BLK), F32),
            jax.ShapeDtypeStruct((I_BLK, RANK), F32),
            jax.ShapeDtypeStruct((J_BLK, RANK), F32),
        ),
        in_specs=[anywhere, anywhere, vmem, vmem, vmem],
        out_specs=(anywhere, vmem, vmem),
        scratch_shapes=[
            f32(ROWS, J_BLK),
            pltpu.VMEM((ROWS, J_BLK), jnp.int32),
            pltpu.VMEM((ROWS, J_BLK), BF16),
            pltpu.VMEM((ROWS, J_BLK), BF16),
            f32(I_BLK, RANK),
            f32(J_BLK, RANK),
            pltpu.VMEM((I_BLK, 3 * RANK), BF16),
            f32(N_GROUP, RANK, GROUP),
            f32(RANK, RANK),
            f32(RANK, RANK),
            f32(RANK, J_BLK),
            f32(N_X * PIECE, RANK),
            f32(N_TM * PIECE, RANK),
            f32(RANK, RANK),
            f32(I_BLK, RANK),
            f32(I_BLK, RANK),
            f32(RANK, I_BLK),
            f32(N_EP * PIECE, RANK),
            f32(N_EP * PIECE, RANK),
            f32(RANK, RANK),
            f32(J_BLK, RANK),
            f32(RANK, J_BLK),
            f32(J_BLK, RANK),
            pltpu.SemaphoreType.DMA((2 * N_GROUP,)),
            pltpu.SemaphoreType.DMA((1,)),
            pltpu.SemaphoreType.DMA((8,)),
            pltpu.SemaphoreType.DMA((8,)),
        ],
        compiler_params=pltpu.CompilerParams(
            collective_id=0, has_side_effects=True, vmem_limit_bytes=VMEM_LIMIT
        ),
        name="fit",
    )(obs, miss, a_own, b_own, channel)


def complete_kernel(w_ref, a_ref, b_ref, chan_ref, out_ref, w_buf, acat, load_sem, save_sem):
    for g in range(N_GROUP):
        rows = pl.ds(g * G_ROWS, G_ROWS)
        pltpu.make_async_copy(w_ref.at[rows], w_buf.at[rows], load_sem.at[g]).start()
    acat[...] = pack_left(a_ref[...])

    def group(g, _):
        settle(w_buf.at[rows_at(g, G_ROWS)], load_sem.at[g])
        for p in range(0, GROUP, 2):
            k = g * GROUP + p
            b_high, b_low = basis_pair(b_ref[...], chan_ref, k)
            model = model_pair(acat[...], b_high, b_low)
            for d in range(2):
                rows = rows_at(k + d, I_BLK)
                w = w_buf[rows, :]
                w_buf[rows, :] = jnp.where(w != w, model[:, d * J_BLK : (d + 1) * J_BLK], w)
        return 0

    for g in range(N_GROUP):
        group(g, 0)
        for q in range(GROUP):
            k = g * GROUP + q
            pltpu.make_async_copy(
                w_buf.at[pl.ds(k * I_BLK, I_BLK)], out_ref.at[:, k, :], save_sem.at[g]
            ).start()
    for g in range(N_GROUP):
        settle(w_buf.at[pl.ds(g * G_ROWS, G_ROWS)], save_sem.at[g])


def complete(w, a_block, b_block, channel):
    vmem = pl.BlockSpec(memory_space=pltpu.VMEM)
    anywhere = pl.BlockSpec(memory_space=pl.ANY)
    return pl.pallas_call(
        complete_kernel,
        out_shape=jax.ShapeDtypeStruct((I_BLK, WIDTH, J_BLK), F32),
        in_specs=[anywhere, vmem, vmem, vmem],
        out_specs=anywhere,
        scratch_shapes=[
            pltpu.VMEM((ROWS, J_BLK), F32),
            pltpu.VMEM((I_BLK, 3 * RANK), BF16),
            pltpu.SemaphoreType.DMA((N_GROUP,)),
            pltpu.SemaphoreType.DMA((N_GROUP,)),
        ],
        compiler_params=pltpu.CompilerParams(vmem_limit_bytes=VMEM_LIMIT),
        name="complete",
    )(w, a_block, b_block, channel)


def on_device(observed, missing, episode_init, time_init, channel):
    obs = observed.transpose(0, 2, 1)
    miss = missing.transpose(0, 2, 1)
    w, a, b = fit(obs, miss, episode_init, time_init, channel)
    return complete(w, a, b, channel).transpose(0, 2, 1)


def solution(mesh):
    in_specs = (
        P("ep", "tm", None),
        P("ep", "tm", None),
        P(("ep", "tm"), None),
        P(("tm", "ep"), None),
        P(),
    )
    return jax.shard_map(
        on_device, mesh=mesh, in_specs=in_specs, out_specs=P("ep", "tm", None), check_vma=False
    )
```

time: 1340 us -> 148 us (0.11)
  waiting for transfers between devices: 819 us -> 0 us
  other arithmetic: 225 us -> 0 us
  blocking collectives: 164 us -> 0 us
  Pallas kernels: 0 us -> 148 us
  matrix products: 64.3 us -> 0 us
  local copies, waits for them, and re-layouts: 38 us -> 0 us
  between operations: 21.1 us -> 0.01 us
    psum x4 -> x0, waiting for transfers between devices: 819 us -> none  [shard_gram(): return lax.psum(gram_rows(own_rows), ('ep', 'tm'))]
    another operation x36 -> x0, other arithmetic: 217 us -> none  [the longest x27 138 us: system_factor(): return jnp.linalg.cholesky(system)]
    all_gather x6 -> x0, blocking collectives: 164 us -> none  [the longest x3 118 us: gather_episode(): return lax.all_gather(rows, 'tm', axis=0, tiled=True)]
    pallas_call x0 -> x2, Pallas kernels: none -> 148 us  [the longest x1 142 us: fit(): pl.pallas_call(fit_kernel, out_shape=(jax.ShapeDtypeStruct((ROWS, J_BLK),...]
    dot_general x12 -> x0, matrix products: 51.3 us -> none  [the longest x2 18.4 us: on_device(): jnp.dot(filled, basis, precision=HIGH, preferred_element_type=jnp.float32)]
    another operation x37 -> x0, local copies, waits for them, and re-layouts: 16.4 us -> none  [the longest x29 16.3 us: solve_rows(): return jax.scipy.linalg.cho_solve((lower, True), moments.T).T]
  transfers between devices with their start and end apart: 8 -> 0, of which waited for: 4 -> 0; matrix products, arithmetic and copies ran while one was open for 22% -> 0% of each run, Pallas kernels for 0% -> 0%
where the time goes in v2:
time: 148 us
  Pallas kernels  148 us (100%)
    pallas_call x1, Pallas kernels, fit(): pl.pallas_call(fit_kernel, out_shape=(jax.ShapeDtypeStruct((ROWS, J_BLK),...  142 us
    pallas_call x1, Pallas kernels, complete(): pl.pallas_call(complete_kernel, out_shape=jax.ShapeDtypeStruct((I_BLK, WI...  5.76 us

profile of v2, /device:TPU:1, one launch (start us, length us, event | category | flops | bytes accessed | tf_op | source)
XLA Modules:
  0.0 148.2 jit_solution(7180233520576355336)
XLA Ops:
  0.0 142.5 %fit.1 = (f32[8192,128]{1,0:T(8,128)}, f32[256,256]{1,0:T(8,128)}, f32[128,256]{1,0:T(8,128)}) custom-call(f32[256,32,128]{2,1,0:T(8,128)} %bitcast.3, s32[256,32,128]{2,1,0:T(8,128)} %bitcast.4, f32[8,256]{1,0:T(8,128)} %a_ref.1, f32[16,256]{1,0:T(8,128)} %b_ref.1, f32[32,256]{1,0:T(8,128)} %chan_ref.3), custom_call_target="tpu_custom_call" | custom-call | tf_op jit(solution)/shard_map/fit/pallas_call | solution.py:471
  142.5 5.8 %complete.1 = f32[256,32,128]{2,1,0:T(8,128)} custom-call(f32[8192,128]{1,0:T(8,128)} %get-tuple-element.8.w_ref, f32[256,256]{1,0:T(8,128)} %get-tuple-element.9.a_ref, f32[128,256]{1,0:T(8,128)} %get-tuple-element.10.b_ref, f32[32,256]{1,0:T(8,128)} %chan_ref.3), custom_call_target="tpu_custom_call" | custom-call | tf_op jit(solution)/shard_map/complete/pallas_call | solution.py:548

commit v3 on v2

--- a/solution.py
+++ b/solution.py
@@ -162,7 +162,10 @@
 
     lax.fori_loop(1, N_TM, along_tm, 0)
     lax.fori_loop(N_X, N_EP * N_X, in_layer, 0)
-    pl.semaphore_wait(barrier, N_TM - 1 + (N_EP - 1) * N_X)
+
+
+def await_greetings():
+    pl.semaphore_wait(pltpu.get_barrier_semaphore(), N_TM - 1 + (N_EP - 1) * N_X)
 
 
 def send_tm(src_of, dst, send_sem, recv_sem):
@@ -279,6 +282,7 @@
     gb_full,
     me_part,
     me_recv,
+    me_full,
     at_buf,
     ga_part,
     ga_recv,
@@ -286,12 +290,14 @@
     mt_part,
     mt_acc,
     mt_recv,
+    mt_full,
     load_sem,
     save_sem,
     send_sem,
     recv_sem,
 ):
     e, t, z, x = coords()
+    greet()
     for g in range(N_GROUP):
         for q in range(GROUP):
             k = g * GROUP + q
@@ -311,16 +317,6 @@
     others_ga_full = ga_full.at[pl.ds(0, (N_EP * N_X - 1) * PIECE)]
     others_mt = mt_recv.at[pl.ds(0, (N_EP - 1) * B_OWN)]
 
-    def send_b():
-        send_ep(lambda peer: b_buf.at[b_mine], b_buf.at[b_mine], send_sem.at[0], recv_sem.at[0])
-
-    def send_a():
-        send_tm(lambda peer: a_buf.at[a_mine], a_buf.at[a_mine], send_sem.at[1], recv_sem.at[1])
-
-    greet()
-    send_b()
-    send_a()
-
     chan_t = chan_ref[...].T
     gram_c[...] = dot_high(chan_t, chan_ref[...])
     for g in range(N_GROUP):
@@ -342,14 +338,15 @@
     lax.fori_loop(0, N_GROUP, mask_group, 0)
     save = pltpu.make_async_copy(w_buf, w_ref, save_sem.at[0])
     save.start()
-    settle(others_a, recv_sem.at[1])
-    settle(others_a, send_sem.at[1])
-
-    def sweep(s, _):
-        acat[...] = pack_left(a_buf[...])
-        me_part[...] = jnp.zeros_like(me_part)
-        settle(others_b, recv_sem.at[0])
-        settle(others_b, send_sem.at[0])
+    await_greetings()
+    send_ep(lambda peer: b_buf.at[b_mine], b_buf.at[b_mine], send_sem.at[0], recv_sem.at[0])
+    send_tm(lambda peer: a_buf.at[a_mine], a_buf.at[a_mine], send_sem.at[1], recv_sem.at[1])
+    me_mine = rows_at(t, A_OWN)
+    mt_mine = rows_at(e, B_OWN)
+    others_me_full = me_full.at[pl.ds(0, (N_TM - 1) * A_OWN)]
+    others_mt_full = mt_full.at[pl.ds(0, (N_EP - 1) * B_OWN)]
+
+    def start_gram_b():
         b = b_buf[...]
         bt_buf[...] = b.T
         gb_part[...] = dot_high(bt_buf[rows_at(e, N_X * PIECE), :], b)
@@ -358,6 +355,16 @@
             lambda peer: gb_part.at[rows_at(peer % N_X, PIECE)], gb_slot, send_sem.at[2], recv_sem.at[2]
         )
         gb_recv[rows_at(t, PIECE), :] = gb_part[rows_at(x, PIECE), :]
+
+    settle(others_b, recv_sem.at[0])
+    start_gram_b()
+    settle(others_a, recv_sem.at[1])
+    acat[...] = pack_left(a_buf[...])
+    settle(others_b, send_sem.at[0])
+    settle(others_a, send_sem.at[1])
+
+    def sweep(s, _):
+        me_part[...] = jnp.zeros_like(me_part)
 
         def episode_group(g, _):
             for p in range(0, GROUP, 2):
@@ -390,19 +397,16 @@
         gb_mine = rows_at(e * N_X + x, PIECE)
         gb_full[gb_mine, :] = sum_slots(gb_recv, N_TM, PIECE)
         send_layer(gb_full.at[gb_mine], gb_full.at[gb_mine], send_sem.at[3], recv_sem.at[3])
+        settle(others_me, recv_sem.at[4])
+        me_full[me_mine, :] = sum_slots(me_recv, N_TM, A_OWN)
+        send_tm(lambda peer: me_full.at[me_mine], me_full.at[me_mine], send_sem.at[8], recv_sem.at[8])
         settle(others_gb_full, recv_sem.at[3])
         form_system(s_buf, gb_full, gram_c)
         invert_in_place(s_buf, RANK, 32)
-        settle(others_me, recv_sem.at[4])
-        a_buf[a_mine, :] = dot_high(sum_slots(me_recv, N_TM, A_OWN), s_buf[...])
-        send_a()
-        settle(others_gb, send_sem.at[2])
-        settle(others_gb_full, send_sem.at[3])
-        settle(others_me, send_sem.at[4])
-
-        settle(others_a, recv_sem.at[1])
-        settle(others_a, send_sem.at[1])
-        a = a_buf[...]
+        settle(others_me_full, recv_sem.at[8])
+        a = dot_high(me_full[...], s_buf[...])
+        a_buf[...] = a
+
         at = a.T
         at_buf[...] = at
         ga_part[...] = dot_high(at_buf[rows_at(x, N_EP * PIECE), :], a)
@@ -410,6 +414,10 @@
         send_ep(lambda peer: ga_part.at[rows_at(peer, PIECE)], ga_slot, send_sem.at[5], recv_sem.at[5])
         ga_recv[rows_at(e, PIECE), :] = ga_part[rows_at(e, PIECE), :]
         acat[...] = pack_left(at_buf[...])
+        settle(others_gb, send_sem.at[2])
+        settle(others_gb_full, send_sem.at[3])
+        settle(others_me, send_sem.at[4])
+        settle(others_me_full, send_sem.at[8])
         mt_acc[...] = jnp.zeros_like(mt_acc)
 
         def time_group(g, _):
@@ -435,21 +443,28 @@
         ga_mine = rows_at(x * N_EP + e, PIECE)
         ga_full[ga_mine, :] = sum_slots(ga_recv, N_EP, PIECE)
         send_layer(ga_full.at[ga_mine], ga_full.at[ga_mine], send_sem.at[6], recv_sem.at[6])
+        settle(others_mt, recv_sem.at[7])
+        mt_full[mt_mine, :] = sum_slots(mt_recv, N_EP, B_OWN)
+        send_ep(lambda peer: mt_full.at[mt_mine], mt_full.at[mt_mine], send_sem.at[9], recv_sem.at[9])
         settle(others_ga_full, recv_sem.at[6])
         form_system(s_buf, ga_full, gram_c)
         invert_in_place(s_buf, RANK, 32)
-        settle(others_mt, recv_sem.at[7])
-        b_buf[b_mine, :] = dot_high(sum_slots(mt_recv, N_EP, B_OWN), s_buf[...])
-        send_b()
+        settle(others_mt_full, recv_sem.at[9])
+        b_buf[...] = dot_high(mt_full[...], s_buf[...])
         settle(others_ga, send_sem.at[5])
         settle(others_ga_full, send_sem.at[6])
         settle(others_mt, send_sem.at[7])
+        settle(others_mt_full, send_sem.at[9])
+
+        @pl.when(s < SWEEPS - 1)
+        def _():
+            start_gram_b()
+            acat[...] = pack_left(a_buf[...])
+
         return 0
 
     lax.fori_loop(0, SWEEPS, sweep, 0)
     aout_ref[...] = a_buf[...]
-    settle(others_b, recv_sem.at[0])
-    settle(others_b, send_sem.at[0])
     bout_ref[...] = b_buf[...]
     save.wait()
 
@@ -494,6 +509,7 @@
             f32(RANK, RANK),
             f32(I_BLK, RANK),
             f32(I_BLK, RANK),
+            f32(I_BLK, RANK),
             f32(RANK, I_BLK),
             f32(N_EP * PIECE, RANK),
             f32(N_EP * PIECE, RANK),
@@ -501,10 +517,11 @@
             f32(J_BLK, RANK),
             f32(RANK, J_BLK),
             f32(J_BLK, RANK),
+            f32(J_BLK, RANK),
             pltpu.SemaphoreType.DMA((2 * N_GROUP,)),
             pltpu.SemaphoreType.DMA((1,)),
-            pltpu.SemaphoreType.DMA((8,)),
-            pltpu.SemaphoreType.DMA((8,)),
+            pltpu.SemaphoreType.DMA((10,)),
+            pltpu.SemaphoreType.DMA((10,)),
         ],
         compiler_params=pltpu.CompilerParams(
             collective_id=0, has_side_effects=True, vmem_limit_bytes=VMEM_LIMIT

time: 148 us -> 122 us (0.82)
  Pallas kernels: 148 us -> 122 us
    pallas_call x1, Pallas kernels: 142 us -> 116 us  [fit(): pl.pallas_call(fit_kernel, out_shape=(jax.ShapeDtypeStruct((ROWS, J_BLK),...]
where the time goes in v3:
time: 122 us
  Pallas kernels  122 us (100%)
    pallas_call x1, Pallas kernels, fit(): pl.pallas_call(fit_kernel, out_shape=(jax.ShapeDtypeStruct((ROWS, J_BLK),...  116 us
    pallas_call x1, Pallas kernels, complete(): pl.pallas_call(complete_kernel, out_shape=jax.ShapeDtypeStruct((I_BLK, WI...  5.76 us

profile of v3, /device:TPU:1, one launch (start us, length us, event | category | flops | bytes accessed | tf_op | source)
XLA Modules:
  0.0 121.9 jit_solution(5520063166259374890)
XLA Ops:
  0.0 116.1 %fit.1 = (f32[8192,128]{1,0:T(8,128)}, f32[256,256]{1,0:T(8,128)}, f32[128,256]{1,0:T(8,128)}) custom-call(f32[256,32,128]{2,1,0:T(8,128)} %bitcast.3, s32[256,32,128]{2,1,0:T(8,128)} %bitcast.4, f32[8,256]{1,0:T(8,128)} %a_ref.1, f32[16,256]{1,0:T(8,128)} %b_ref.1, f32[32,256]{1,0:T(8,128)} %chan_ref.3), custom_call_target="tpu_custom_call" | custom-call | tf_op jit(solution)/shard_map/fit/pallas_call | solution.py:486
  116.1 5.8 %complete.1 = f32[256,32,128]{2,1,0:T(8,128)} custom-call(f32[8192,128]{1,0:T(8,128)} %get-tuple-element.8.w_ref, f32[256,256]{1,0:T(8,128)} %get-tuple-element.9.a_ref, f32[128,256]{1,0:T(8,128)} %get-tuple-element.10.b_ref, f32[32,256]{1,0:T(8,128)} %chan_ref.3), custom_call_target="tpu_custom_call" | custom-call | tf_op jit(solution)/shard_map/complete/pallas_call | solution.py:565

commit v4 on v3

--- a/solution.py
+++ b/solution.py
@@ -26,6 +26,9 @@
 A_OWN = 8
 B_OWN = 16
 PIECE = 8
+HALF = 128
+PANEL = 32
+N_PIECE = N_EP * N_X
 VMEM_LIMIT = 56 * 1024 * 1024
 
 
@@ -126,17 +129,23 @@
             ref[r0 + 8 * v : r0 + 8 * v + 8, 128 * t : 128 * t + 128] = x[v][t]
 
 
-def invert_in_place(ref, n, depth):
-    for k in range(n // depth):
-        r0 = k * depth
-        eliminate_panel(ref, r0, depth, n)
-        panel = ref[r0 : r0 + depth, :]
-        lane = lax.broadcasted_iota(jnp.int32, (1, n), 1)
-        inside = (lane >= r0) & (lane < r0 + depth)
-        for lo, hi in ((0, r0), (r0 + depth, n)):
+def eliminate_rows(ref, lo, hi, r0, depth):
+    n = ref.shape[1]
+    lane = lax.broadcasted_iota(jnp.int32, (1, n), 1)
+    inside = (lane >= r0) & (lane < r0 + depth)
+    product = dot_packed(ref[lo:hi, r0 : r0 + depth], ref[r0 : r0 + depth, :])
+    ref[lo:hi, :] = jnp.where(inside, 0.0, ref[lo:hi, :]) - product
+
+
+def eliminate_half(ref, base, depth, between=None):
+    top = base + HALF
+    for r0 in range(base, top, depth):
+        eliminate_panel(ref, r0, depth, ref.shape[1])
+        for lo, hi in ((base, r0), (r0 + depth, top)):
             if hi > lo:
-                cols = ref[lo:hi, r0 : r0 + depth]
-                ref[lo:hi, :] = jnp.where(inside, 0.0, ref[lo:hi, :]) - dot_packed(cols, panel)
+                eliminate_rows(ref, lo, hi, r0, depth)
+        if between is not None and r0 == base + depth:
+            between()
 
 
 def coords():
@@ -310,11 +319,11 @@
     b_buf[b_mine, :] = b_ref[...]
     others_a = a_buf.at[pl.ds(0, (N_TM - 1) * A_OWN)]
     others_b = b_buf.at[pl.ds(0, (N_EP - 1) * B_OWN)]
-    others_gb = gb_recv.at[pl.ds(0, (N_TM - 1) * PIECE)]
-    others_gb_full = gb_full.at[pl.ds(0, (N_EP * N_X - 1) * PIECE)]
+    others_gb = [gb_recv.at[h, pl.ds(0, (N_TM - 1) * PIECE)] for h in range(2)]
+    others_gb_full = [gb_full.at[h, pl.ds(0, (N_PIECE - 1) * PIECE)] for h in range(2)]
     others_me = me_recv.at[pl.ds(0, (N_TM - 1) * A_OWN)]
-    others_ga = ga_recv.at[pl.ds(0, (N_EP - 1) * PIECE)]
-    others_ga_full = ga_full.at[pl.ds(0, (N_EP * N_X - 1) * PIECE)]
+    others_ga = [ga_recv.at[h, pl.ds(0, (N_EP - 1) * PIECE)] for h in range(2)]
+    others_ga_full = [ga_full.at[h, pl.ds(0, (N_PIECE - 1) * PIECE)] for h in range(2)]
     others_mt = mt_recv.at[pl.ds(0, (N_EP - 1) * B_OWN)]
 
     chan_t = chan_ref[...].T
@@ -349,12 +358,16 @@
     def start_gram_b():
         b = b_buf[...]
         bt_buf[...] = b.T
-        gb_part[...] = dot_high(bt_buf[rows_at(e, N_X * PIECE), :], b)
-        gb_slot = gb_recv.at[rows_at(t, PIECE)]
-        send_tm(
-            lambda peer: gb_part.at[rows_at(peer % N_X, PIECE)], gb_slot, send_sem.at[2], recv_sem.at[2]
-        )
-        gb_recv[rows_at(t, PIECE), :] = gb_part[rows_at(x, PIECE), :]
+        for h in range(2):
+            slab = pl.ds(pl.multiple_of(h * HALF + e * 2 * PIECE, PIECE), 2 * PIECE)
+            store_pieces(gb_part, h, dot_high(bt_buf[slab, :], b))
+            send_tm(
+                lambda peer: gb_part.at[h, rows_at(peer % N_X, PIECE)],
+                gb_recv.at[h, rows_at(t, PIECE)],
+                send_sem.at[2 + h],
+                recv_sem.at[2 + h],
+            )
+            gb_recv[h, rows_at(t, PIECE), :] = gb_part[h, rows_at(x, PIECE), :]
 
     settle(others_b, recv_sem.at[0])
     start_gram_b()
@@ -391,33 +404,49 @@
 
         lax.fori_loop(0, N_GROUP, episode_group, 0)
         me_slot = me_recv.at[rows_at(t, A_OWN)]
-        send_tm(lambda peer: me_part.at[rows_at(peer, A_OWN)], me_slot, send_sem.at[4], recv_sem.at[4])
+        send_tm(lambda peer: me_part.at[rows_at(peer, A_OWN)], me_slot, send_sem.at[6], recv_sem.at[6])
         me_recv[rows_at(t, A_OWN), :] = me_part[rows_at(t, A_OWN), :]
-        settle(others_gb, recv_sem.at[2])
         gb_mine = rows_at(e * N_X + x, PIECE)
-        gb_full[gb_mine, :] = sum_slots(gb_recv, N_TM, PIECE)
-        send_layer(gb_full.at[gb_mine], gb_full.at[gb_mine], send_sem.at[3], recv_sem.at[3])
-        settle(others_me, recv_sem.at[4])
-        me_full[me_mine, :] = sum_slots(me_recv, N_TM, A_OWN)
-        send_tm(lambda peer: me_full.at[me_mine], me_full.at[me_mine], send_sem.at[8], recv_sem.at[8])
-        settle(others_gb_full, recv_sem.at[3])
-        form_system(s_buf, gb_full, gram_c)
-        invert_in_place(s_buf, RANK, 32)
-        settle(others_me_full, recv_sem.at[8])
+        for h in range(2):
+            settle(others_gb[h], recv_sem.at[2 + h])
+            gb_full[h, gb_mine, :] = sum_slots(gb_recv.at[h], N_TM, PIECE)
+            mine = gb_full.at[h, gb_mine]
+            send_layer(mine, mine, send_sem.at[4 + h], recv_sem.at[4 + h])
+        settle(others_gb_full[0], recv_sem.at[4])
+        form_half(s_buf, gb_full, gram_c, 0)
+
+        def share_me():
+            settle(others_me, recv_sem.at[6])
+            me_full[me_mine, :] = sum_slots(me_recv, N_TM, A_OWN)
+            mine = me_full.at[me_mine]
+            send_tm(lambda peer: mine, mine, send_sem.at[7], recv_sem.at[7])
+
+        eliminate_half(s_buf, 0, PANEL, share_me)
+        settle(others_gb_full[1], recv_sem.at[5])
+        form_half(s_buf, gb_full, gram_c, 1)
+        finish_inverse(s_buf)
+        settle(others_me_full, recv_sem.at[7])
         a = dot_high(me_full[...], s_buf[...])
         a_buf[...] = a
 
         at = a.T
         at_buf[...] = at
-        ga_part[...] = dot_high(at_buf[rows_at(x, N_EP * PIECE), :], a)
-        ga_slot = ga_recv.at[rows_at(e, PIECE)]
-        send_ep(lambda peer: ga_part.at[rows_at(peer, PIECE)], ga_slot, send_sem.at[5], recv_sem.at[5])
-        ga_recv[rows_at(e, PIECE), :] = ga_part[rows_at(e, PIECE), :]
+        for h in range(2):
+            slab = pl.ds(pl.multiple_of(h * HALF + x * 4 * PIECE, PIECE), 4 * PIECE)
+            store_pieces(ga_part, h, dot_high(at_buf[slab, :], a))
+            send_ep(
+                lambda peer: ga_part.at[h, rows_at(peer, PIECE)],
+                ga_recv.at[h, rows_at(e, PIECE)],
+                send_sem.at[8 + h],
+                recv_sem.at[8 + h],
+            )
+            ga_recv[h, rows_at(e, PIECE), :] = ga_part[h, rows_at(e, PIECE), :]
         acat[...] = pack_left(at_buf[...])
-        settle(others_gb, send_sem.at[2])
-        settle(others_gb_full, send_sem.at[3])
-        settle(others_me, send_sem.at[4])
-        settle(others_me_full, send_sem.at[8])
+        for h in range(2):
+            settle(others_gb[h], send_sem.at[2 + h])
+            settle(others_gb_full[h], send_sem.at[4 + h])
+        settle(others_me, send_sem.at[6])
+        settle(others_me_full, send_sem.at[7])
         mt_acc[...] = jnp.zeros_like(mt_acc)
 
         def time_group(g, _):
@@ -437,24 +466,30 @@
         lax.fori_loop(0, N_GROUP, time_group, 0)
         mt_part[...] = mt_acc[...].T
         mt_slot = mt_recv.at[rows_at(e, B_OWN)]
-        send_ep(lambda peer: mt_part.at[rows_at(peer, B_OWN)], mt_slot, send_sem.at[7], recv_sem.at[7])
+        send_ep(lambda peer: mt_part.at[rows_at(peer, B_OWN)], mt_slot, send_sem.at[12], recv_sem.at[12])
         mt_recv[rows_at(e, B_OWN), :] = mt_part[rows_at(e, B_OWN), :]
-        settle(others_ga, recv_sem.at[5])
         ga_mine = rows_at(x * N_EP + e, PIECE)
-        ga_full[ga_mine, :] = sum_slots(ga_recv, N_EP, PIECE)
-        send_layer(ga_full.at[ga_mine], ga_full.at[ga_mine], send_sem.at[6], recv_sem.at[6])
-        settle(others_mt, recv_sem.at[7])
+        for h in range(2):
+            settle(others_ga[h], recv_sem.at[8 + h])
+            ga_full[h, ga_mine, :] = sum_slots(ga_recv.at[h], N_EP, PIECE)
+            mine = ga_full.at[h, ga_mine]
+            send_layer(mine, mine, send_sem.at[10 + h], recv_sem.at[10 + h])
+        settle(others_mt, recv_sem.at[12])
         mt_full[mt_mine, :] = sum_slots(mt_recv, N_EP, B_OWN)
-        send_ep(lambda peer: mt_full.at[mt_mine], mt_full.at[mt_mine], send_sem.at[9], recv_sem.at[9])
-        settle(others_ga_full, recv_sem.at[6])
-        form_system(s_buf, ga_full, gram_c)
-        invert_in_place(s_buf, RANK, 32)
-        settle(others_mt_full, recv_sem.at[9])
+        send_ep(lambda peer: mt_full.at[mt_mine], mt_full.at[mt_mine], send_sem.at[13], recv_sem.at[13])
+        settle(others_ga_full[0], recv_sem.at[10])
+        form_half(s_buf, ga_full, gram_c, 0)
+        eliminate_half(s_buf, 0, PANEL)
+        settle(others_ga_full[1], recv_sem.at[11])
+        form_half(s_buf, ga_full, gram_c, 1)
+        finish_inverse(s_buf)
+        settle(others_mt_full, recv_sem.at[13])
         b_buf[...] = dot_high(mt_full[...], s_buf[...])
-        settle(others_ga, send_sem.at[5])
-        settle(others_ga_full, send_sem.at[6])
-        settle(others_mt, send_sem.at[7])
-        settle(others_mt_full, send_sem.at[9])
+        for h in range(2):
+            settle(others_ga[h], send_sem.at[8 + h])
+            settle(others_ga_full[h], send_sem.at[10 + h])
+        settle(others_mt, send_sem.at[12])
+        settle(others_mt_full, send_sem.at[13])
 
         @pl.when(s < SWEEPS - 1)
         def _():
@@ -469,11 +504,25 @@
     save.wait()
 
 
-def form_system(s_ref, gram_ref, gram_c):
-    eye = lax.broadcasted_iota(jnp.int32, (RANK, RANK), 0) == lax.broadcasted_iota(
-        jnp.int32, (RANK, RANK), 1
-    )
-    s_ref[...] = gram_ref[...] * gram_c[...] + jnp.where(eye, RIDGE, 0.0)
+def store_pieces(ref, h, rows):
+    for p in range(2 * rows.shape[0] // PIECE):
+        r, c = PIECE * (p // 2), HALF * (p % 2)
+        ref[h, PIECE * p : PIECE * (p + 1), :] = rows[r : r + PIECE, c : c + HALF]
+
+
+def form_half(s_ref, gram_ref, gram_c, h):
+    row = lax.broadcasted_iota(jnp.int32, (PIECE, HALF), 0)
+    lane = lax.broadcasted_iota(jnp.int32, (PIECE, HALF), 1)
+    for p in range(N_PIECE):
+        r, c = h * HALF + PIECE * (p // 2), HALF * (p % 2)
+        part = gram_ref[h, PIECE * p : PIECE * (p + 1), :] * gram_c[r : r + PIECE, c : c + HALF]
+        s_ref[r : r + PIECE, c : c + HALF] = part + jnp.where(row + r == lane + c, RIDGE, 0.0)
+
+
+def finish_inverse(s_ref):
+    eliminate_rows(s_ref, HALF, RANK, 0, HALF)
+    eliminate_half(s_ref, HALF, PANEL)
+    eliminate_rows(s_ref, 0, HALF, HALF, HALF)
 
 
 def fit(obs, miss, a_own, b_own, channel):
@@ -504,24 +553,24 @@
             f32(RANK, RANK),
             f32(RANK, RANK),
             f32(RANK, J_BLK),
-            f32(N_X * PIECE, RANK),
-            f32(N_TM * PIECE, RANK),
-            f32(RANK, RANK),
+            f32(2, N_X * PIECE, HALF),
+            f32(2, N_TM * PIECE, HALF),
+            f32(2, N_PIECE * PIECE, HALF),
             f32(I_BLK, RANK),
             f32(I_BLK, RANK),
             f32(I_BLK, RANK),
             f32(RANK, I_BLK),
-            f32(N_EP * PIECE, RANK),
-            f32(N_EP * PIECE, RANK),
-            f32(RANK, RANK),
+            f32(2, N_EP * PIECE, HALF),
+            f32(2, N_EP * PIECE, HALF),
+            f32(2, N_PIECE * PIECE, HALF),
             f32(J_BLK, RANK),
             f32(RANK, J_BLK),
             f32(J_BLK, RANK),
             f32(J_BLK, RANK),
             pltpu.SemaphoreType.DMA((2 * N_GROUP,)),
             pltpu.SemaphoreType.DMA((1,)),
-            pltpu.SemaphoreType.DMA((10,)),
-            pltpu.SemaphoreType.DMA((10,)),
+            pltpu.SemaphoreType.DMA((14,)),
+            pltpu.SemaphoreType.DMA((14,)),
         ],
         compiler_params=pltpu.CompilerParams(
             collective_id=0, has_side_effects=True, vmem_limit_bytes=VMEM_LIMIT

time: 122 us -> 122 us (level)
  no operation moved by 1% of the time
where the time goes in v4:
time: 122 us
  Pallas kernels  122 us (100%)
    pallas_call x1, Pallas kernels, fit(): pl.pallas_call(fit_kernel, out_shape=(jax.ShapeDtypeStruct((ROWS, J_BLK),...  116 us
    pallas_call x1, Pallas kernels, complete(): pl.pallas_call(complete_kernel, out_shape=jax.ShapeDtypeStruct((I_BLK, WI...  5.76 us

profile of v4, /device:TPU:1, one launch (start us, length us, event | category | flops | bytes accessed | tf_op | source)
XLA Modules:
  0.0 122.1 jit_solution(9986899683844787597)
XLA Ops:
  0.0 116.3 %fit.1 = (f32[8192,128]{1,0:T(8,128)}, f32[256,256]{1,0:T(8,128)}, f32[128,256]{1,0:T(8,128)}) custom-call(f32[256,32,128]{2,1,0:T(8,128)} %bitcast.3, s32[256,32,128]{2,1,0:T(8,128)} %bitcast.4, f32[8,256]{1,0:T(8,128)} %a_ref.1, f32[16,256]{1,0:T(8,128)} %b_ref.1, f32[32,256]{1,0:T(8,128)} %chan_ref.3), custom_call_target="tpu_custom_call" | custom-call | tf_op jit(solution)/shard_map/fit/pallas_call | solution.py:535
  116.3 5.8 %complete.1 = f32[256,32,128]{2,1,0:T(8,128)} custom-call(f32[8192,128]{1,0:T(8,128)} %get-tuple-element.8.w_ref, f32[256,256]{1,0:T(8,128)} %get-tuple-element.9.a_ref, f32[128,256]{1,0:T(8,128)} %get-tuple-element.10.b_ref, f32[32,256]{1,0:T(8,128)} %chan_ref.3), custom_call_target="tpu_custom_call" | custom-call | tf_op jit(solution)/shard_map/complete/pallas_call | solution.py:614

commit v5 on v4

--- a/solution.py
+++ b/solution.py
@@ -27,7 +27,7 @@
 B_OWN = 16
 PIECE = 8
 HALF = 128
-PANEL = 32
+PANEL = 16
 N_PIECE = N_EP * N_X
 VMEM_LIMIT = 56 * 1024 * 1024
 
@@ -144,7 +144,7 @@
         for lo, hi in ((base, r0), (r0 + depth, top)):
             if hi > lo:
                 eliminate_rows(ref, lo, hi, r0, depth)
-        if between is not None and r0 == base + depth:
+        if between is not None and r0 == base + 3 * depth:
             between()
 
 
@@ -358,9 +358,8 @@
     def start_gram_b():
         b = b_buf[...]
         bt_buf[...] = b.T
+        store_slab(gb_part, bt_buf, e, 2 * PIECE, b)
         for h in range(2):
-            slab = pl.ds(pl.multiple_of(h * HALF + e * 2 * PIECE, PIECE), 2 * PIECE)
-            store_pieces(gb_part, h, dot_high(bt_buf[slab, :], b))
             send_tm(
                 lambda peer: gb_part.at[h, rows_at(peer % N_X, PIECE)],
                 gb_recv.at[h, rows_at(t, PIECE)],
@@ -431,9 +430,8 @@
 
         at = a.T
         at_buf[...] = at
+        store_slab(ga_part, at_buf, x, 4 * PIECE, a)
         for h in range(2):
-            slab = pl.ds(pl.multiple_of(h * HALF + x * 4 * PIECE, PIECE), 4 * PIECE)
-            store_pieces(ga_part, h, dot_high(at_buf[slab, :], a))
             send_ep(
                 lambda peer: ga_part.at[h, rows_at(peer, PIECE)],
                 ga_recv.at[h, rows_at(e, PIECE)],
@@ -504,10 +502,19 @@
     save.wait()
 
 
-def store_pieces(ref, h, rows):
-    for p in range(2 * rows.shape[0] // PIECE):
-        r, c = PIECE * (p // 2), HALF * (p % 2)
-        ref[h, PIECE * p : PIECE * (p + 1), :] = rows[r : r + PIECE, c : c + HALF]
+def store_slab(ref, turned, index, count, factor):
+    rows = jnp.concatenate(
+        [
+            turned[pl.ds(pl.multiple_of(h * HALF + index * count, PIECE), count), :]
+            for h in range(2)
+        ],
+        axis=0,
+    )
+    gram = dot_high(rows, factor)
+    for h in range(2):
+        for p in range(2 * count // PIECE):
+            r, c = h * count + PIECE * (p // 2), HALF * (p % 2)
+            ref[h, PIECE * p : PIECE * (p + 1), :] = gram[r : r + PIECE, c : c + HALF]
 
 
 def form_half(s_ref, gram_ref, gram_c, h):
@@ -585,25 +592,17 @@
         pltpu.make_async_copy(w_ref.at[rows], w_buf.at[rows], load_sem.at[g]).start()
     acat[...] = pack_left(a_ref[...])
 
-    def group(g, _):
-        settle(w_buf.at[rows_at(g, G_ROWS)], load_sem.at[g])
+    for g in range(N_GROUP):
+        settle(w_buf.at[pl.ds(g * G_ROWS, G_ROWS)], load_sem.at[g])
         for p in range(0, GROUP, 2):
             k = g * GROUP + p
             b_high, b_low = basis_pair(b_ref[...], chan_ref, k)
             model = model_pair(acat[...], b_high, b_low)
             for d in range(2):
-                rows = rows_at(k + d, I_BLK)
+                rows = pl.ds((k + d) * I_BLK, I_BLK)
                 w = w_buf[rows, :]
                 w_buf[rows, :] = jnp.where(w != w, model[:, d * J_BLK : (d + 1) * J_BLK], w)
-        return 0
-
-    for g in range(N_GROUP):
-        group(g, 0)
-        for q in range(GROUP):
-            k = g * GROUP + q
-            pltpu.make_async_copy(
-                w_buf.at[pl.ds(k * I_BLK, I_BLK)], out_ref.at[:, k, :], save_sem.at[g]
-            ).start()
+                pltpu.make_async_copy(w_buf.at[rows], out_ref.at[:, k + d, :], save_sem.at[g]).start()
     for g in range(N_GROUP):
         settle(w_buf.at[pl.ds(g * G_ROWS, G_ROWS)], save_sem.at[g])
 

time: 122 us -> 121 us (level)
    pallas_call x1, Pallas kernels: 116 us -> 115 us  [fit(): pl.pallas_call(fit_kernel, out_shape=(jax.ShapeDtypeStruct((ROWS, J_BLK),...]
where the time goes in v5:
time: 121 us
  Pallas kernels  121 us (100%)
    pallas_call x1, Pallas kernels, fit(): pl.pallas_call(fit_kernel, out_shape=(jax.ShapeDtypeStruct((ROWS, J_BLK),...  115 us
    pallas_call x1, Pallas kernels, complete(): pl.pallas_call(complete_kernel, out_shape=jax.ShapeDtypeStruct((I_BLK, WI...  5.97 us

profile of v5, /device:TPU:1, one launch (start us, length us, event | category | flops | bytes accessed | tf_op | source)
XLA Modules:
  0.0 121.0 jit_solution(3164934359710425009)
XLA Ops:
  0.0 114.9 %fit.1 = (f32[8192,128]{1,0:T(8,128)}, f32[256,256]{1,0:T(8,128)}, f32[128,256]{1,0:T(8,128)}) custom-call(f32[256,32,128]{2,1,0:T(8,128)} %bitcast.3, s32[256,32,128]{2,1,0:T(8,128)} %bitcast.4, f32[8,256]{1,0:T(8,128)} %a_ref.1, f32[16,256]{1,0:T(8,128)} %b_ref.1, f32[32,256]{1,0:T(8,128)} %chan_ref.3), custom_call_target="tpu_custom_call" | custom-call | tf_op jit(solution)/shard_map/fit/pallas_call | solution.py:542
  114.9 6.0 %complete.1 = f32[256,32,128]{2,1,0:T(8,128)} custom-call(f32[8192,128]{1,0:T(8,128)} %get-tuple-element.8.w_ref, f32[256,256]{1,0:T(8,128)} %get-tuple-element.9.a_ref, f32[128,256]{1,0:T(8,128)} %get-tuple-element.10.b_ref, f32[32,256]{1,0:T(8,128)} %chan_ref.3), custom_call_target="tpu_custom_call" | custom-call | tf_op jit(solution)/shard_map/complete/pallas_call | solution.py:613

commit v6 on v5

--- a/solution.py
+++ b/solution.py
@@ -319,7 +319,7 @@
     b_buf[b_mine, :] = b_ref[...]
     others_a = a_buf.at[pl.ds(0, (N_TM - 1) * A_OWN)]
     others_b = b_buf.at[pl.ds(0, (N_EP - 1) * B_OWN)]
-    others_gb = [gb_recv.at[h, pl.ds(0, (N_TM - 1) * PIECE)] for h in range(2)]
+    others_gb = gb_recv.at[pl.ds(0, (N_TM - 1) * 2 * PIECE)]
     others_gb_full = [gb_full.at[h, pl.ds(0, (N_PIECE - 1) * PIECE)] for h in range(2)]
     others_me = me_recv.at[pl.ds(0, (N_TM - 1) * A_OWN)]
     others_ga = [ga_recv.at[h, pl.ds(0, (N_EP - 1) * PIECE)] for h in range(2)]
@@ -358,15 +358,20 @@
     def start_gram_b():
         b = b_buf[...]
         bt_buf[...] = b.T
-        store_slab(gb_part, bt_buf, e, 2 * PIECE, b)
-        for h in range(2):
-            send_tm(
-                lambda peer: gb_part.at[h, rows_at(peer % N_X, PIECE)],
-                gb_recv.at[h, rows_at(t, PIECE)],
-                send_sem.at[2 + h],
-                recv_sem.at[2 + h],
-            )
-            gb_recv[h, rows_at(t, PIECE), :] = gb_part[h, rows_at(x, PIECE), :]
+        gram = slab_gram(bt_buf, e, 2 * PIECE, b)
+        for p in range(N_X):
+            for h in range(2):
+                r, c = h * 2 * PIECE + PIECE * (p // 2), HALF * (p % 2)
+                to = PIECE * (2 * p + h)
+                gb_part[to : to + PIECE, :] = gram[r : r + PIECE, c : c + HALF]
+        slot = rows_at(t, 2 * PIECE)
+        send_tm(
+            lambda peer: gb_part.at[rows_at(peer % N_X, 2 * PIECE)],
+            gb_recv.at[slot],
+            send_sem.at[2],
+            recv_sem.at[2],
+        )
+        gb_recv[slot, :] = gb_part[rows_at(x, 2 * PIECE), :]
 
     settle(others_b, recv_sem.at[0])
     start_gram_b()
@@ -406,9 +411,10 @@
         send_tm(lambda peer: me_part.at[rows_at(peer, A_OWN)], me_slot, send_sem.at[6], recv_sem.at[6])
         me_recv[rows_at(t, A_OWN), :] = me_part[rows_at(t, A_OWN), :]
         gb_mine = rows_at(e * N_X + x, PIECE)
+        settle(others_gb, recv_sem.at[2])
+        both = sum_slots(gb_recv, N_TM, 2 * PIECE)
         for h in range(2):
-            settle(others_gb[h], recv_sem.at[2 + h])
-            gb_full[h, gb_mine, :] = sum_slots(gb_recv.at[h], N_TM, PIECE)
+            gb_full[h, gb_mine, :] = both[h * PIECE : (h + 1) * PIECE, :]
             mine = gb_full.at[h, gb_mine]
             send_layer(mine, mine, send_sem.at[4 + h], recv_sem.at[4 + h])
         settle(others_gb_full[0], recv_sem.at[4])
@@ -440,8 +446,8 @@
             )
             ga_recv[h, rows_at(e, PIECE), :] = ga_part[h, rows_at(e, PIECE), :]
         acat[...] = pack_left(at_buf[...])
+        settle(others_gb, send_sem.at[2])
         for h in range(2):
-            settle(others_gb[h], send_sem.at[2 + h])
             settle(others_gb_full[h], send_sem.at[4 + h])
         settle(others_me, send_sem.at[6])
         settle(others_me_full, send_sem.at[7])
@@ -503,6 +509,14 @@
 
 
 def store_slab(ref, turned, index, count, factor):
+    gram = slab_gram(turned, index, count, factor)
+    for h in range(2):
+        for p in range(2 * count // PIECE):
+            r, c = h * count + PIECE * (p // 2), HALF * (p % 2)
+            ref[h, PIECE * p : PIECE * (p + 1), :] = gram[r : r + PIECE, c : c + HALF]
+
+
+def slab_gram(turned, index, count, factor):
     rows = jnp.concatenate(
         [
             turned[pl.ds(pl.multiple_of(h * HALF + index * count, PIECE), count), :]
@@ -510,11 +524,7 @@
         ],
         axis=0,
     )
-    gram = dot_high(rows, factor)
-    for h in range(2):
-        for p in range(2 * count // PIECE):
-            r, c = h * count + PIECE * (p // 2), HALF * (p % 2)
-            ref[h, PIECE * p : PIECE * (p + 1), :] = gram[r : r + PIECE, c : c + HALF]
+    return dot_high(rows, factor)
 
 
 def form_half(s_ref, gram_ref, gram_c, h):
@@ -560,8 +570,8 @@
             f32(RANK, RANK),
             f32(RANK, RANK),
             f32(RANK, J_BLK),
-            f32(2, N_X * PIECE, HALF),
-            f32(2, N_TM * PIECE, HALF),
+            f32(N_X * 2 * PIECE, HALF),
+            f32(N_TM * 2 * PIECE, HALF),
             f32(2, N_PIECE * PIECE, HALF),
             f32(I_BLK, RANK),
             f32(I_BLK, RANK),

time: 121 us -> 123 us (1.017)
  Pallas kernels: 121 us -> 123 us
    pallas_call x1, Pallas kernels: 115 us -> 117 us  [fit(): pl.pallas_call(fit_kernel, out_shape=(jax.ShapeDtypeStruct((ROWS, J_BLK),...]
where the time goes in v6:
time: 123 us
  Pallas kernels  123 us (100%)
    pallas_call x1, Pallas kernels, fit(): pl.pallas_call(fit_kernel, out_shape=(jax.ShapeDtypeStruct((ROWS, J_BLK),...  117 us
    pallas_call x1, Pallas kernels, complete(): pl.pallas_call(complete_kernel, out_shape=jax.ShapeDtypeStruct((I_BLK, WI...  5.97 us

profile of v6, /device:TPU:1, one launch (start us, length us, event | category | flops | bytes accessed | tf_op | source)
XLA Modules:
  0.0 122.8 jit_solution(7475652266407231768)
XLA Ops:
  0.0 116.6 %fit.1 = (f32[8192,128]{1,0:T(8,128)}, f32[256,256]{1,0:T(8,128)}, f32[128,256]{1,0:T(8,128)}) custom-call(f32[256,32,128]{2,1,0:T(8,128)} %bitcast.3, s32[256,32,128]{2,1,0:T(8,128)} %bitcast.4, f32[8,256]{1,0:T(8,128)} %a_ref.1, f32[16,256]{1,0:T(8,128)} %b_ref.1, f32[32,256]{1,0:T(8,128)} %chan_ref.3), custom_call_target="tpu_custom_call" | custom-call | tf_op jit(solution)/shard_map/fit/pallas_call | solution.py:552
  116.6 6.0 %complete.1 = f32[256,32,128]{2,1,0:T(8,128)} custom-call(f32[8192,128]{1,0:T(8,128)} %get-tuple-element.8.w_ref, f32[256,256]{1,0:T(8,128)} %get-tuple-element.9.a_ref, f32[128,256]{1,0:T(8,128)} %get-tuple-element.10.b_ref, f32[32,256]{1,0:T(8,128)} %chan_ref.3), custom_call_target="tpu_custom_call" | custom-call | tf_op jit(solution)/shard_map/complete/pallas_call | solution.py:623
